TPU v7x, 256 devices: a whole 4x4x8 slice. The times are simulated.
256 devices in a mesh: outer: 32 (over y_lo, z, core), inner: 8 (over x, y_hi).
Axes of the slice: x: 4, y: 4 (y_hi: 2, y_lo: 2; y = y_hi * 2 + y_lo), z: 8, core: 2. Of those that a mesh axis runs over, the one named last changes fastest.
Arguments:
- queries: bfloat16 [131072, 1024], P(('outer', 'inner')), may hold values from -12 to 12
- keys: bfloat16 [131072, 1024], P(('outer', 'inner')), may hold values from -12 to 12
- values: bfloat16 [131072, 1024], P(('outer', 'inner')), may hold values from -6 to 6
Outputs:
- attended: bfloat16 [131072, 1024], P(('outer', 'inner'))
All inputs are finite; a program needn't handle non-finite values.
Results may differ from a plain program's by a relative error of at most 0.0031.
Values may be sent and summed in bfloat16 or wider, within the bound.
A program may use at most 128 MiB of HBM per device.

v0:
```python
import jax
import jax.numpy as jnp
from jax import lax
from jax.sharding import PartitionSpec as P

DEVICE_TOKENS = 512
HEADS = 16
HEAD_SIZE = 64
WIDTH = 1024


lowest_score = -1e30


def select_rows(rows, stride):
    count = rows.shape[0] // stride
    shaped = rows.reshape(count, stride, rows.shape[1], rows.shape[2])
    chosen = jnp.arange(stride)[:, None] == (jnp.arange(rows.shape[1]) % stride)[None, :]
    return jnp.sum(jnp.where(chosen[None, :, :, None], shaped, jnp.zeros((), rows.dtype)), axis=1)


def head_scores(queries, keys):
    return jnp.einsum(
        "zof,sof->ozs", queries, keys, preferred_element_type=jnp.float32
    ) * queries.shape[-1] ** (-0.5)


def attend_group(queries, keys, values):
    logit_matrix = head_scores(queries, keys)
    top = jnp.max(logit_matrix, axis=-1, keepdims=True)
    exponent_scores = jnp.exp(logit_matrix - top)
    total = jnp.sum(exponent_scores, axis=-1)
    merged_output = jnp.einsum(
        "yeg,gyt->eyt",
        exponent_scores.astype(jnp.bfloat16),
        values,
        preferred_element_type=jnp.float32,
    )
    att = merged_output / jnp.transpose(total)[:, :, None]
    lse = top[..., 0] + jnp.log(total)
    return (att, jnp.transpose(lse))


def attend_local(queries, keys, values):
    heads = queries.shape[1]
    group = min(4, heads)
    results = []
    scales = []
    for first in range(0, heads, group):
        att, lse = attend_group(
            queries[:, first : first + group],
            keys[:, first : first + group],
            values[:, first : first + group],
        )
        results.append(att)
        scales.append(lse)
    return (jnp.concatenate(results, axis=1), jnp.concatenate(scales, axis=1))


def fold_start(queries):
    heads = queries.shape[1]
    count = queries.shape[0]
    return (
        jnp.full((heads, count), lowest_score, jnp.float32),
        jnp.zeros((heads, count), jnp.float32),
        jnp.zeros(queries.shape, jnp.float32),
    )


def fold_for(queries, carry, piece):
    heads = queries.shape[1]
    size = queries.shape[2]
    top, total, acc = carry
    key_piece = piece[0].reshape(piece[0].shape[0], heads, size)
    value_segment = piece[1].reshape(piece[1].shape[0], heads, size)
    logit_matrix = head_scores(queries, key_piece)
    new_top = jnp.maximum(top, jnp.max(logit_matrix, axis=-1))
    exponent_scores = jnp.exp(logit_matrix - new_top[..., None])
    total = jnp.sum(exponent_scores, axis=-1)
    added = jnp.einsum(
        "yeg,gyt->eyt",
        exponent_scores.astype(jnp.bfloat16),
        value_segment,
        preferred_element_type=jnp.float32,
    )
    acc = added
    return (new_top, total, acc)


def fold_finish(carry):
    top, total, acc = carry
    att = acc / jnp.transpose(total)[:, :, None]
    return (att, jnp.transpose(top + jnp.log(total)))


def spread_rows(att, lse, stride):
    count = att.shape[0]
    heads = att.shape[1]
    chosen = jnp.arange(stride)[:, None] == (jnp.arange(heads) % stride)[None, :]
    full_att = jnp.where(chosen[None, :, :, None], att[:, None], jnp.zeros((), jnp.float32))
    full_lse = jnp.where(chosen[None, :, :], lse[:, None], jnp.full((), lowest_score, jnp.float32))
    return (
        full_att.reshape(count * stride, heads, att.shape[2]),
        full_lse.reshape(count * stride, heads),
    )


def merge_levels(parts):
    highest = parts[0][1]
    for pair in parts[1:]:
        highest = jnp.maximum(highest, pair[1])
    numer = jnp.zeros(parts[0][0].shape, jnp.float32)
    denom = jnp.zeros(highest.shape, jnp.float32)
    for att, lse in parts:
        weight = jnp.exp(lse - highest)
        numer = numer + weight[:, :, None] * att
        denom = denom + weight
    return numer / denom[:, :, None]


def on_device(queries, keys, values):
    inner_size = lax.axis_size("inner")
    all_size = lax.axis_size("outer") * inner_size
    local_q = queries.reshape(DEVICE_TOKENS, HEADS, HEAD_SIZE)
    local_k = keys.reshape(DEVICE_TOKENS, HEADS, HEAD_SIZE)
    local_v = values.reshape(DEVICE_TOKENS, HEADS, HEAD_SIZE)
    mid_q = select_rows(local_q, inner_size)
    mid_k = select_rows(local_k, inner_size)
    mid_v = select_rows(local_v, inner_size)
    mid_rows = mid_q.shape[0]
    carry = fold_for(
        mid_q,
        fold_start(mid_q),
        (
            lax.all_gather(mid_k.reshape(mid_rows, WIDTH), "inner", axis=0, tiled=True),
            lax.all_gather(mid_v.reshape(mid_rows, WIDTH), "inner", axis=0, tiled=True),
        ),
    )
    mid_att, mid_lse = fold_finish(carry)
    far_q = select_rows(local_q, all_size)
    far_k = select_rows(local_k, all_size)
    far_v = select_rows(local_v, all_size)
    far_rows = far_q.shape[0]
    carry = fold_for(
        far_q,
        fold_start(far_q),
        (
            lax.all_gather(far_k.reshape(far_rows, WIDTH), ("outer", "inner"), axis=0, tiled=True),
            lax.all_gather(far_v.reshape(far_rows, WIDTH), ("outer", "inner"), axis=0, tiled=True),
        ),
    )
    far_att, far_lse = fold_finish(carry)
    first = attend_local(local_q, local_k, local_v)
    second = spread_rows(mid_att, mid_lse, inner_size)
    third = spread_rows(far_att, far_lse, all_size)
    merged = merge_levels([first, second, third])
    return merged.astype(jnp.bfloat16).reshape(DEVICE_TOKENS, WIDTH)


def solution(mesh):
    in_specs = (
        P(("outer", "inner"), None),
        P(("outer", "inner"), None),
        P(("outer", "inner"), None),
    )
    out_specs = P(("outer", "inner"), None)
    return jax.shard_map(
        on_device, mesh=mesh, in_specs=in_specs, out_specs=out_specs, check_vma=False
    )
```

profile of v0, /device:TPU:1, one launch (start us, length us, event | category | flops | bytes accessed | tf_op | source)
XLA Modules:
  0.0 1210.6 jit_solution(18206066329473286125)
XLA Ops:
  6.6 3.0 reshape_reshape.22
  9.5 4.1 reshape_reshape.19
  13.7 2.3 reshape_reshape.18
  16.0 5.5 select_reduce_fusion
  21.5 1.8 reshape.356
  26.3 2.3 copy.127
  32.3 5.5 fusion.70
  37.8 1.7 copy.146
  39.7 1.7 copy.147
  46.5 1.6 fusion.46
  48.1 1.7 fusion.49
  50.6 1.7 fusion.52
  53.0 1.6 fusion.55
  54.8 24.0 %all-gather.7.cloned.1.call-done = bf16[512,1024]{1,0:T(8,128)(2,1)} async-done(((bf16[64,1024]{1,0:T(8,128)(2,1)}), bf16[512,1024]{1,0:T(8,128)(2,1)}) %all-gather.7.cloned.1.call-update) | async-done | bytes 1048592 | tf_op jit(solution)/shard_map/all_gather | solution.py:135
  82.5 50.2 %all-gather.9.cloned.1.call-done = bf16[512,1024]{1,0:T(8,128)(2,1)} async-done(((bf16[64,1024]{1,0:T(8,128)(2,1)}), bf16[512,1024]{1,0:T(8,128)(2,1)}) %all-gather.9.cloned.1.call-update) | async-done | bytes 1048592 | tf_op jit(solution)/shard_map/all_gather | solution.py:136
  137.0 2.3 broadcast_in_dim.217
  139.2 4.9 broadcast_in_dim.218
  144.1 1.9 copy.135
  146.0 518.2 %all-gather.11.cloned.1.call-done = bf16[256,2,1024]{2,1,0:T(2,128)(2,1)} async-done(((bf16[1,2,1024]{2,1,0:T(2,128)(2,1)}), bf16[256,2,1024]{2,1,0:T(2,128)(2,1)}) %all-gather.11.cloned.1.call-update) | async-done | bytes 1048592 | tf_op jit(solution)/shard_map/all_gather | solution.py:148
  664.2 4.8 reshape.359
  669.0 2.5 fusion.96
  671.9 519.6 %all-gather.13.cloned.1.call-done = bf16[256,2,1024]{2,1,0:T(2,128)(2,1)} async-done(((bf16[1,2,1024]{2,1,0:T(2,128)(2,1)}), bf16[256,2,1024]{2,1,0:T(2,128)(2,1)}) %all-gather.13.cloned.1.call-update) | async-done | bytes 1048592 | tf_op jit(solution)/shard_map/all_gather | solution.py:149
  1191.5 4.8 reshape.364
  1196.2 2.3 fusion.64
  (67 shorter events, 27.2 us)
Async XLA Ops:
  6.5 72.2 %all-gather.7.cloned.1.call-start = ((), (), s32[]{:S(2)}) async-start(), calls=%async_computation | async-start | bytes 1179648 | tf_op jit(solution)/shard_map/all_gather | solution.py:135
  9.5 4.2 copy-start
  23.3 109.5 %all-gather.9.cloned.1.call-start = ((), (), s32[]{:S(2)}) async-start(), calls=%async_computation.1 | async-start | bytes 1179648 | tf_op jit(solution)/shard_map/all_gather | solution.py:136
  24.2 640.0 %all-gather.11.cloned.1.call-start = ((), (), s32[]{:S(2)}) async-start(), calls=%async_computation.2 | async-start | bytes 1052672 | tf_op jit(solution)/shard_map/all_gather | solution.py:148
  39.5 1151.9 %all-gather.13.cloned.1.call-start = ((), (), s32[]{:S(2)}) async-start(), calls=%async_computation.3 | async-start | bytes 1052672 | tf_op jit(solution)/shard_map/all_gather | solution.py:149
  45.3 1.2 copy-start.1
  1200.0 1.0 copy-start.2
  1200.0 1.2 copy-start.3
  1200.1 1.3 copy-start.4
  1200.1 1.5 copy-start.5
Sparse Core Ops, SparseCore 0:
  23.4 55.3 all-gather.6
  81.4 51.3 all-gather.8
  134.6 529.6 all-gather.10
  665.9 525.5 all-gather.12
where the time goes:
time: 1210 us
  waiting for transfers between devices  1110 us (92%)
  local copies, waits for them, and re-layouts  51.4 us (4%)
  matrix products  17.4 us (1%)
  other arithmetic  16 us (1%)
  between operations  13.4 us (1%)
    all_gather x1, waiting for transfers between devices, on_device(): lax.all_gather(far_v.reshape(far_rows, WIDTH), ('outer', 'inner'), axis=0...  520 us
    all_gather x1, waiting for transfers between devices, on_device(): lax.all_gather(far_k.reshape(far_rows, WIDTH), ('outer', 'inner'), axis=0...  518 us
    all_gather x1, waiting for transfers between devices, on_device(): lax.all_gather(mid_v.reshape(mid_rows, WIDTH), 'inner', axis=0, tiled=True)  50.2 us
  transfers between devices with their start and end apart: 4, of which 4 were waited for; matrix products, arithmetic and copies ran while one was open for 5% of the time, Pallas kernels for 0%

commit v1 on v0

v1 whole, which is shorter than its diff:
```python
import jax
import jax.numpy as jnp
from jax import lax
from jax.experimental import pallas as pl
from jax.experimental.pallas import tpu as pltpu
from jax.sharding import PartitionSpec as P

MESH = pl.DeviceIdType.MESH
F32 = jnp.float32
BF16 = jnp.bfloat16

ROWS = 512
PAIRS = 8
MID = 64
FAR = 2
INNER = 8
RG = 16
GG = 16
BACK = MID + 16
LOWEST = -1e30

INNER_STEPS = ((2, 1), (1, 1), (3, 1), (2, 0), (0, 1), (1, 0), (3, 0))
Z_STEPS = (4, 3, 5, 2, 6, 1, 7, 0)


def lane_is_second(shape):
    return lax.broadcasted_iota(jnp.int32, shape, len(shape) - 1) >= 64


def split_pair(q):
    second = lane_is_second(q.shape)
    zero = jnp.zeros((), q.dtype)
    return jnp.concatenate([jnp.where(second, zero, q), jnp.where(second, q, zero)], axis=0)


def value_block(v):
    second = lane_is_second(v.shape)
    zero = jnp.zeros((), v.dtype)
    one = jnp.ones((), v.dtype)
    first = jnp.concatenate([jnp.where(second, zero, v), jnp.where(second, zero, one)], axis=1)
    other = jnp.concatenate([jnp.where(second, v, zero), jnp.where(second, one, zero)], axis=1)
    return jnp.concatenate([first, other], axis=0)


def scores_of(q, k):
    return lax.dot_general(split_pair(q), k, (((1,), (1,)), ((), ())), preferred_element_type=F32)


def finish(s, block):
    n = s.shape[0] // 2
    top = jnp.max(s, axis=1, keepdims=True)
    prob = jnp.exp(s - top).astype(BF16)
    both = jnp.concatenate([prob[:n], prob[n:]], axis=1)
    out = jnp.dot(both, block, preferred_element_type=F32)
    total = out[:, 128:]
    second = lane_is_second((n, 128))
    return out[:, :128] / total, jnp.where(second, top[n:], top[:n]) + jnp.log(total)


def parts_of(x):
    high = x.astype(BF16)
    rest = x - high.astype(F32)
    mid = rest.astype(BF16)
    return high, mid, (rest - mid.astype(F32)).astype(BF16)


def pack_lse(lse, groups, width):
    high, mid, low = (p.astype(F32) for p in parts_of(lse))
    lane = lax.broadcasted_iota(jnp.int32, (16, 128), 1) % 64
    out = jnp.zeros((16, 128), F32)
    for g in range(groups):
        rows = slice(16 * g, 16 * g + 16)
        for t, part in enumerate((high, mid, low)):
            out = jnp.where(lane == g * width + t, part[rows], out)
    return out.astype(BF16)


def unpack_lse(packed, groups, width):
    row = lax.broadcasted_iota(jnp.int32, (128, 128), 0)
    lane = lax.broadcasted_iota(jnp.int32, (128, 128), 1)
    out = []
    for g in range(groups):
        at = row % 64 - g * width
        take = jnp.logical_and(jnp.logical_and(at >= 0, at < 3), row // 64 == lane // 64)
        out.append(jnp.dot(packed, jnp.where(take, 1.0, 0.0).astype(BF16), preferred_element_type=F32))
    return out


def wait_some(sem, count):
    @pl.when(count > 0)
    def _():
        pl.semaphore_wait(sem, count)


def kernel(
    q_hbm, k_hbm, v_hbm, out_ref,
    q_ref, k_ref, v_ref, edge, load_sem, edge_sem,
    stage, far_stage, mid_send, mid_recv, mid_ssem, mid_rsem,
    back_send, back_recv, back_ssem, back_rsem,
    kv_send, kv_recv, kv_ssem, kv_rsem,
    fq_send, fq_recv, fq_ssem, fq_rsem,
    far_send, far_recv, far_ssem, far_rsem,
    near_sem, along_sem, att_ref, lse_pair, lse_ref, far_att, far_lse,
):
    outer = lax.axis_index("outer")
    inner = lax.axis_index("inner")
    core = outer % 2
    z = (outer // 2) % 8
    y_lo = outer // 16
    x = inner // 2
    y_hi = inner % 2

    def rank(x, y_hi, y_lo, z, core):
        y = y_hi * 2 + y_lo
        hops = x - 2 * (x // 3) + y - 2 * (y // 3) + z - (z // 4) * (z - 4)
        return hops * 256 + (y_lo * 16 + z * 2 + core) * 8 + x * 2 + y_hi

    mine = rank(x, y_hi, y_lo, z, core)

    def outer_id(y_lo, z, core):
        return y_lo * 16 + z * 2 + core

    near = []
    for dc in range(2):
        for dx, dy in INNER_STEPS + ((0, 0),):
            if dc or dx or dy:
                px, py, pc = (x + dx) % 4, (y_hi + dy) % 2, (core + dc) % 2
                near.append(((outer_id(y_lo, z, pc), px * 2 + py), rank(px, py, y_lo, z, pc)))
    along = []
    for dz in Z_STEPS:
        for dy in range(2):
            if dz or dy:
                pz, py = (z + dz) % 8, (y_lo + dy) % 2
                along.append(((outer_id(py, pz, core), inner), rank(x, y_hi, py, pz, core)))

    barrier = pltpu.get_barrier_semaphore()
    lower_near = jnp.int32(0)
    lower_along = jnp.int32(0)
    for who, its in near:
        @pl.when(its > mine)
        def _(who=who):
            pl.semaphore_signal(barrier, 1, device_id=who, device_id_type=MESH)
        lower_near = lower_near + jnp.where(its < mine, 1, 0)
    for who, its in along:
        @pl.when(its > mine)
        def _(who=who):
            pl.semaphore_signal(barrier, 1, device_id=who, device_id_type=MESH)
        lower_along = lower_along + jnp.where(its < mine, 1, 0)

    edges = []
    for a, src in enumerate((q_hbm, k_hbm, v_hbm)):
        for t in range(FAR):
            copy = pltpu.make_async_copy(src.at[pl.ds(256 * t, 16), :], edge.at[a, t], edge_sem.at[a, t])
            copy.start()
            edges.append(copy)
    loads = []
    for a, (src, dst) in enumerate(((q_hbm, q_ref), (k_hbm, k_ref), (v_hbm, v_ref))):
        copy = pltpu.make_async_copy(src, dst, load_sem.at[a])
        copy.start()
        loads.append(copy)

    for copy in edges:
        copy.wait()
    row16 = lax.broadcasted_iota(jnp.int32, (16, 1024), 0)
    head16 = lax.broadcasted_iota(jnp.int32, (16, 1024), 1) // 64
    for a in range(3):
        for t in range(FAR):
            block = edge[a, t].astype(F32)
            if a == 0:
                block = block * 0.125
            picked = jnp.sum(jnp.where(row16 == head16, block, 0.0), axis=0, keepdims=True)
            for p in range(PAIRS):
                far_stage[a, pl.ds(2 * p + t, 1), :] = picked[:, 128 * p : 128 * p + 128]
    fq_send[...] = far_stage[0].astype(BF16)
    kv_send[0:16, :] = far_stage[1].astype(BF16)
    kv_send[16:32, :] = far_stage[2].astype(BF16)
    my_near = core * 8 + inner
    my_along = y_lo * 8 + z
    fq_recv[my_near] = fq_send[...]
    kv_recv[my_along] = kv_send[...]

    wait_some(barrier, lower_near + lower_along)
    for who, its in near:
        @pl.when(its < mine)
        def _(who=who):
            pl.semaphore_signal(near_sem, 1, device_id=who, device_id_type=MESH)
    for who, its in along:
        @pl.when(its < mine)
        def _(who=who):
            pl.semaphore_signal(along_sem, 1, device_id=who, device_id_type=MESH)

    def kv_copy(who):
        return pltpu.make_async_remote_copy(
            src_ref=kv_send, dst_ref=kv_recv.at[my_along], send_sem=kv_ssem, recv_sem=kv_rsem,
            device_id=who, device_id_type=MESH,
        )

    for who, its in along:
        @pl.when(its < mine)
        def _(who=who):
            kv_copy(who).start()

    for copy in loads:
        copy.wait()
    second = lane_is_second((MID, 128))

    def select_pair(p):
        first_row = (2 * p) % 8
        columns = pl.ds(pl.multiple_of(p * 128, 128), 128)
        for a, ref in enumerate((q_ref, k_ref, v_ref)):
            wide = ref[:, columns].astype(F32)
            if a == 0:
                wide = wide * 0.125
            stage[a] = wide
        for a in range(3):
            one = stage[a, pl.ds(first_row, MID, stride=8), :]
            two = stage[a, pl.ds(first_row + 1, MID, stride=8), :]
            mid_send[p, pl.ds(MID * a, MID), :] = jnp.where(second, two, one).astype(BF16)

    def pick(p, carry):
        select_pair(p)
        return carry

    lax.fori_loop(0, PAIRS, pick, 0)
    mid_recv[inner] = mid_send[inner]

    def send_near():
        wait_some(near_sem, 15 - lower_near)
        for dx, dy in INNER_STEPS:
            p = ((x + dx) % 4) * 2 + (y_hi + dy) % 2
            pltpu.make_async_remote_copy(
                src_ref=mid_send.at[p], dst_ref=mid_recv.at[inner], send_sem=mid_ssem, recv_sem=mid_rsem,
                device_id=(outer, p), device_id_type=MESH,
            ).start()
        for who, _ in near:
            pltpu.make_async_remote_copy(
                src_ref=fq_send, dst_ref=fq_recv.at[my_near], send_sem=fq_ssem, recv_sem=fq_rsem,
                device_id=who, device_id_type=MESH,
            ).start()

    def send_along():
        wait_some(along_sem, 15 - lower_along)
        for who, its in along:
            @pl.when(its > mine)
            def _(who=who):
                kv_copy(who).start()

    def middle():
        got = mid_recv.at[pl.ds(0, INNER - 1)]
        pltpu.make_async_copy(got, got, mid_rsem).wait()
        keys = mid_recv[:, MID : 2 * MID, :].reshape(ROWS, 128)
        block = value_block(mid_recv[:, 2 * MID :, :].reshape(ROWS, 128))
        for half in range(4):
            q = mid_recv[2 * half : 2 * half + 2, 0:MID, :].reshape(128, 128)
            att, lse = finish(scores_of(q, keys), block)
            for s in range(2):
                rows = slice(MID * s, MID * s + MID)
                back_send[2 * half + s, 0:MID, :] = att[rows].astype(BF16)
                back_send[2 * half + s, MID:BACK, :] = pack_lse(lse[rows], 4, 16)
        for dx, dy in INNER_STEPS:
            p = ((x + dx) % 4) * 2 + (y_hi + dy) % 2
            pltpu.make_async_remote_copy(
                src_ref=back_send.at[p], dst_ref=back_recv.at[inner], send_sem=back_ssem, recv_sem=back_rsem,
                device_id=(outer, p), device_id_type=MESH,
            ).start()
        back_recv[inner] = back_send[inner]

    def far():
        got = kv_recv.at[pl.ds(0, GG - 1)]
        pltpu.make_async_copy(got, got, kv_rsem).wait()
        got = fq_recv.at[pl.ds(0, RG - 1)]
        pltpu.make_async_copy(got, got, fq_rsem).wait()
        stage[0] = kv_recv[...].reshape(ROWS, 128).astype(F32)
        stage[1, 0:256, :] = fq_recv[...].reshape(256, 128).astype(F32)
        scores, blocks = [], []
        for p in range(PAIRS):
            q = jnp.concatenate([stage[1, pl.ds(2 * p + t, RG, stride=16), :] for t in range(FAR)], axis=0)
            k = jnp.concatenate([stage[0, pl.ds(2 * p + t, GG, stride=32), :] for t in range(FAR)], axis=0)
            v = jnp.concatenate([stage[0, pl.ds(16 + 2 * p + t, GG, stride=32), :] for t in range(FAR)], axis=0)
            scores.append(scores_of(q.astype(BF16), k.astype(BF16)))
            blocks.append(value_block(v.astype(BF16)))
        for p in range(PAIRS):
            att, lse = finish(scores[p], blocks[p])
            for t in range(FAR):
                far_att[pl.ds(2 * p + t, RG, stride=16), :] = att[RG * t : RG * t + RG]
                far_lse[pl.ds(2 * p + t, RG, stride=16), :] = lse[RG * t : RG * t + RG]
        for s in range(RG):
            far_send[s, 0:16, :] = far_att[16 * s : 16 * s + 16, :].astype(BF16)
            far_send[s, 16:32, :] = pack_lse(far_lse[16 * s : 16 * s + 16, :], 1, 16)
        for (o, i), _ in near:
            pltpu.make_async_remote_copy(
                src_ref=far_send.at[(o % 2) * 8 + i], dst_ref=far_recv.at[my_near],
                send_sem=far_ssem, recv_sem=far_rsem, device_id=(o, i), device_id_type=MESH,
            ).start()
        far_recv[my_near] = far_send[my_near]

    def first_level(p):
        columns = pl.ds(pl.multiple_of(p * 128, 128), 128)
        keys = k_ref[:, columns]
        block = value_block(v_ref[:, columns])
        for c in range(4):
            rows = pl.ds(128 * c, 128)
            q = q_ref[rows, columns] * jnp.asarray(0.125, BF16)
            att, lse = finish(scores_of(q, keys), block)
            att_ref[p, rows, :] = att
            lse_pair[rows, :] = lse
        first_row = (2 * p) % 8
        one = lse_pair[pl.ds(first_row, MID, stride=8), :]
        two = lse_pair[pl.ds(first_row + 1, MID, stride=8), :]
        lse_ref[p] = jnp.where(second, two, one)

    hops = mine // 256
    at_near = jnp.where(hops >= 6, 0, jnp.where(hops >= 3, 1, 2))
    at_along = at_near + 1
    at_mid = at_near + 3
    at_far = at_near + 5

    def step(t, carry):
        @pl.when(t == at_near)
        def _():
            send_near()

        @pl.when(t == at_along)
        def _():
            send_along()

        @pl.when(t == at_mid)
        def _():
            middle()

        @pl.when(t == at_far)
        def _():
            far()

        @pl.when(t < PAIRS)
        def _():
            first_level(t)

        return carry

    lax.fori_loop(0, PAIRS + 1, step, 0)

    got = back_recv.at[pl.ds(0, INNER - 1)]
    pltpu.make_async_copy(got, got, back_rsem).wait()
    got = far_recv.at[pl.ds(0, RG - 1)]
    pltpu.make_async_copy(got, got, far_rsem).wait()

    partial_lse = unpack_lse(far_recv[:, 16:32, :].reshape(256, 128), 1, 16)[0]
    top = partial_lse[0:16]
    for s in range(1, RG):
        top = jnp.maximum(top, partial_lse[16 * s : 16 * s + 16])
    numer = jnp.zeros((16, 128), F32)
    denom = jnp.zeros((16, 128), F32)
    for s in range(RG):
        weight = jnp.exp(partial_lse[16 * s : 16 * s + 16] - top)
        numer = numer + weight * far_recv[s, 0:16, :].astype(F32)
        denom = denom + weight
    far_att[0:16, :] = numer / denom
    far_lse[0:16, :] = top + jnp.log(denom)

    mid_lse = unpack_lse(back_recv[:, MID:BACK, :].reshape(128, 128), 4, 16)
    for p in range(PAIRS):
        first_row = (2 * p) % 8
        one = att_ref[p, pl.ds(first_row, MID, stride=8), :]
        two = att_ref[p, pl.ds(first_row + 1, MID, stride=8), :]
        att1 = jnp.where(second, two, one)
        lse1 = lse_ref[p]
        att2 = back_recv[p, 0:MID, :].astype(F32)
        lse2 = jnp.concatenate([mid_lse[g][16 * p : 16 * p + 16] for g in range(4)], axis=0)
        row = lax.broadcasted_iota(jnp.int32, (MID, 128), 0)
        att3 = jnp.zeros((MID, 128), F32)
        lse3 = jnp.full((MID, 128), LOWEST, F32)
        for t in range(FAR):
            here = row == 32 * t + p // 4
            att3 = jnp.where(here, far_att[2 * p + t : 2 * p + t + 1, :], att3)
            lse3 = jnp.where(here, far_lse[2 * p + t : 2 * p + t + 1, :], lse3)
        top = jnp.maximum(jnp.maximum(lse1, lse2), lse3)
        w1, w2, w3 = jnp.exp(lse1 - top), jnp.exp(lse2 - top), jnp.exp(lse3 - top)
        merged = (w1 * att1 + w2 * att2 + w3 * att3) / (w1 + w2 + w3)
        att_ref[p, pl.ds(first_row, MID, stride=8), :] = jnp.where(second, one, merged)
        att_ref[p, pl.ds(first_row + 1, MID, stride=8), :] = jnp.where(second, merged, two)
        out_ref[:, 128 * p : 128 * p + 128] = att_ref[p].astype(BF16)

    sent = mid_send.at[pl.ds(0, INNER - 1)]
    pltpu.make_async_copy(sent, sent, mid_ssem).wait()
    sent = back_send.at[pl.ds(0, INNER - 1)]
    pltpu.make_async_copy(sent, sent, back_ssem).wait()
    sent = kv_recv.at[pl.ds(0, GG - 1)]
    pltpu.make_async_copy(sent, sent, kv_ssem).wait()
    sent = fq_recv.at[pl.ds(0, RG - 1)]
    pltpu.make_async_copy(sent, sent, fq_ssem).wait()
    sent = far_send.at[pl.ds(0, RG - 1)]
    pltpu.make_async_copy(sent, sent, far_ssem).wait()


def on_device(queries, keys, values):
    dma = pltpu.SemaphoreType.DMA
    vmem = pltpu.VMEM
    return pl.pallas_call(
        kernel,
        out_shape=jax.ShapeDtypeStruct((ROWS, 1024), BF16),
        in_specs=[pl.BlockSpec(memory_space=pl.ANY)] * 3,
        out_specs=pl.BlockSpec(memory_space=pltpu.VMEM),
        scratch_shapes=[
            vmem((ROWS, 1024), BF16), vmem((ROWS, 1024), BF16), vmem((ROWS, 1024), BF16),
            vmem((3, FAR, 16, 1024), BF16), dma((3,)), dma((3, FAR)),
            vmem((3, ROWS, 128), F32), vmem((3, 16, 128), F32),
            vmem((INNER, 3 * MID, 128), BF16), vmem((INNER, 3 * MID, 128), BF16), dma, dma,
            vmem((INNER, BACK, 128), BF16), vmem((INNER, BACK, 128), BF16), dma, dma,
            vmem((32, 128), BF16), vmem((GG, 32, 128), BF16), dma, dma,
            vmem((16, 128), BF16), vmem((RG, 16, 128), BF16), dma, dma,
            vmem((RG, 32, 128), BF16), vmem((RG, 32, 128), BF16), dma, dma,
            pltpu.SemaphoreType.REGULAR, pltpu.SemaphoreType.REGULAR,
            vmem((PAIRS, ROWS, 128), F32), vmem((ROWS, 128), F32), vmem((PAIRS, MID, 128), F32),
            vmem((256, 128), F32), vmem((256, 128), F32),
        ],
        compiler_params=pltpu.CompilerParams(
            collective_id=0, has_side_effects=True, vmem_limit_bytes=40 * 1024 * 1024
        ),
    )(queries, keys, values)


def solution(mesh):
    spec = P(("outer", "inner"), None)
    return jax.shard_map(
        on_device, mesh=mesh, in_specs=(spec, spec, spec), out_specs=spec, check_vma=False
    )
```

time: 1210 us -> 31.7 us (0.03)
  waiting for transfers between devices: 1110 us -> 0 us
  local copies, waits for them, and re-layouts: 51.4 us -> 4.65 us
  Pallas kernels: 0 us -> 26.8 us
  matrix products: 17.4 us -> 0 us
  other arithmetic: 16 us -> 0 us
  between operations: 13.4 us -> 0.01 us
    all_gather x4 -> x0, waiting for transfers between devices: 1110 us -> none  [the longest x1 520 us: on_device(): lax.all_gather(far_v.reshape(far_rows, WIDTH), ('outer', 'inner'), axis=0...]
    pallas_call x0 -> x1, Pallas kernels: none -> 26.8 us  [on_device(): pl.pallas_call(kernel, out_shape=jax.ShapeDtypeStruct((ROWS, 1024), BF16)...]
    dot_general x12 -> x0, matrix products: 17.4 us -> none  [the longest x6 7.04 us: head_scores(): jnp.einsum('zof,sof->ozs', queries, keys, preferred_element_type=jnp.floa...]
    reduce_sum x8 -> x0, other arithmetic: 14.6 us -> none  [the longest x2 11 us: select_rows(): jnp.sum(jnp.where(chosen[None, :, :, None], shaped, jnp.zeros((), rows.dt...]
    another operation x6 -> x0, local copies, waits for them, and re-layouts: 13 us -> none  [select_rows(): shaped = rows.reshape(count, stride, rows.shape[1], rows.shape[2])]
    reshape x4 -> x0, local copies, waits for them, and re-layouts: 12.2 us -> none  [the longest x1 4.78 us: fold_for(): key_piece = piece[0].reshape(piece[0].shape[0], heads, size)]
  transfers between devices with their start and end apart: 4 -> 0, of which waited for: 4 -> 0; matrix products, arithmetic and copies ran while one was open for 5% -> 0% of each run, Pallas kernels for 0% -> 0%
where the time goes in v1:
time: 31.7 us; the launch traced here: 31.5 us
  Pallas kernels  26.8 us (85%)
  local copies, waits for them, and re-layouts  4.65 us (15%)
    pallas_call x1, Pallas kernels, on_device(): pl.pallas_call(kernel, out_shape=jax.ShapeDtypeStruct((ROWS, 1024), BF16)...  26.8 us
    unnamed x7, local copies, waits for them, and re-layouts  4.65 us

profile of v1, /device:TPU:1, one launch (start us, length us, event | category | flops | bytes accessed | tf_op | source)
XLA Modules:
  0.0 31.5 jit_solution(6925940578376446769)
XLA Ops:
  0.0 0.0 copy-start
  0.0 1.2 %copy-done = bf16[512,1024]{1,0:T(8,128)(2,1)S(1)} copy-done((bf16[512,1024]{1,0:T(8,128)(2,1)S(1)}, bf16[512,1024]{1,0:T(8,128)(2,1)}, u32[]{:S(2)}) %copy-start) | copy-done | bytes 1048600
  1.2 0.0 copy-start.1
  1.2 1.2 %copy-done.1 = bf16[512,1024]{1,0:T(8,128)(2,1)S(1)} copy-done((bf16[512,1024]{1,0:T(8,128)(2,1)S(1)}, bf16[512,1024]{1,0:T(8,128)(2,1)}, u32[]{:S(2)}) %copy-start.1) | copy-done | bytes 1048600
  2.5 0.0 copy-start.2
  2.5 1.2 %copy-done.2 = bf16[512,1024]{1,0:T(8,128)(2,1)S(1)} copy-done((bf16[512,1024]{1,0:T(8,128)(2,1)S(1)}, bf16[512,1024]{1,0:T(8,128)(2,1)}, u32[]{:S(2)}) %copy-start.2) | copy-done | bytes 1048600
  3.7 26.8 %shard_map.37 = bf16[512,1024]{1,0:T(8,128)(2,1)S(1)} custom-call(bf16[512,1024]{1,0:T(8,128)(2,1)S(1)} %copy-done, bf16[512,1024]{1,0:T(8,128)(2,1)S(1)} %copy-done.1, bf16[512,1024]{1,0:T(8,128)(2,1)S(1)} %copy-done.2), custom_call_target="tpu_custom_call" | custom-call | tf_op jit(solution)/shard_map/pallas_call | solution.py:399
  30.5 1.0 %copy.5 = bf16[512,1024]{1,0:T(8,128)(2,1)} copy(bf16[512,1024]{1,0:T(8,128)(2,1)S(1)} %shard_map.37) | data formatting | bytes 2097152
Async XLA Ops:
  0.0 1.2 %copy-start = (bf16[512,1024]{1,0:T(8,128)(2,1)S(1)}, bf16[512,1024]{1,0:T(8,128)(2,1)}, u32[]{:S(2)}) copy-start(bf16[512,1024]{1,0:T(8,128)(2,1)} %q_hbm.1) | copy-start | bytes 3145732
  1.2 1.2 %copy-start.1 = (bf16[512,1024]{1,0:T(8,128)(2,1)S(1)}, bf16[512,1024]{1,0:T(8,128)(2,1)}, u32[]{:S(2)}) copy-start(bf16[512,1024]{1,0:T(8,128)(2,1)} %k_hbm.1) | copy-start | bytes 3145732
  2.5 1.2 %copy-start.2 = (bf16[512,1024]{1,0:T(8,128)(2,1)S(1)}, bf16[512,1024]{1,0:T(8,128)(2,1)}, u32[]{:S(2)}) copy-start(bf16[512,1024]{1,0:T(8,128)(2,1)} %v_hbm.1) | copy-start | bytes 3145732

commit v2 on v1

--- a/solution.py
+++ b/solution.py
@@ -18,8 +18,10 @@
 GG = 16
 BACK = MID + 16
 LOWEST = -1e30
-
-INNER_STEPS = ((2, 1), (1, 1), (3, 1), (2, 0), (0, 1), (1, 0), (3, 0))
+STORES = 8
+
+INNER_STEPS = ((2, 2), (1, 2), (3, 2), (2, 0), (0, 2), (1, 0), (3, 0))
+REST_STEPS = ((2, 1), (2, 3), (1, 1), (1, 3), (3, 1), (3, 3), (0, 1), (0, 3))
 Z_STEPS = (4, 3, 5, 2, 6, 1, 7, 0)
 
 
@@ -100,7 +102,7 @@
     kv_send, kv_recv, kv_ssem, kv_rsem,
     fq_send, fq_recv, fq_ssem, fq_rsem,
     far_send, far_recv, far_ssem, far_rsem,
-    near_sem, along_sem, att_ref, lse_pair, lse_ref, far_att, far_lse,
+    along_sem, att_ref, lse_pair, lse_ref, far_att, far_lse,
 ):
     outer = lax.axis_index("outer")
     inner = lax.axis_index("inner")
@@ -110,45 +112,25 @@
     x = inner // 2
     y_hi = inner % 2
 
-    def rank(x, y_hi, y_lo, z, core):
-        y = y_hi * 2 + y_lo
-        hops = x - 2 * (x // 3) + y - 2 * (y // 3) + z - (z // 4) * (z - 4)
-        return hops * 256 + (y_lo * 16 + z * 2 + core) * 8 + x * 2 + y_hi
-
-    mine = rank(x, y_hi, y_lo, z, core)
+    y = y_hi * 2 + y_lo
 
     def outer_id(y_lo, z, core):
         return y_lo * 16 + z * 2 + core
 
-    near = []
-    for dc in range(2):
-        for dx, dy in INNER_STEPS + ((0, 0),):
-            if dc or dx or dy:
-                px, py, pc = (x + dx) % 4, (y_hi + dy) % 2, (core + dc) % 2
-                near.append(((outer_id(y_lo, z, pc), px * 2 + py), rank(px, py, y_lo, z, pc)))
-    along = []
+    near, along = [], []
+    for dx, dy in INNER_STEPS + REST_STEPS:
+        px, py = (x + dx) % 4, (y + dy) % 4
+        near.append((outer_id(py % 2, z, core), px * 2 + py // 2))
+    wave = jnp.minimum(z, 4)
     for dz in Z_STEPS:
-        for dy in range(2):
-            if dz or dy:
-                pz, py = (z + dz) % 8, (y_lo + dy) % 2
-                along.append(((outer_id(py, pz, core), inner), rank(x, y_hi, py, pz, core)))
-
-    barrier = pltpu.get_barrier_semaphore()
-    lower_near = jnp.int32(0)
-    lower_along = jnp.int32(0)
-    for who, its in near:
-        @pl.when(its > mine)
-        def _(who=who):
-            pl.semaphore_signal(barrier, 1, device_id=who, device_id_type=MESH)
-        lower_near = lower_near + jnp.where(its < mine, 1, 0)
-    for who, its in along:
-        @pl.when(its > mine)
-        def _(who=who):
-            pl.semaphore_signal(barrier, 1, device_id=who, device_id_type=MESH)
-        lower_along = lower_along + jnp.where(its < mine, 1, 0)
+        for dc in range(2):
+            if dz or dc:
+                pz = (z + dz) % 8
+                along.append(((outer_id(y_lo, pz, (core + dc) % 2), inner), jnp.minimum(pz, 4) - wave))
+    early_along = jnp.where(z < 4, 2 * z + 1, 15)
 
     edges = []
-    for a, src in enumerate((q_hbm, k_hbm, v_hbm)):
+    for a, src in ((1, k_hbm), (2, v_hbm), (0, q_hbm)):
         for t in range(FAR):
             copy = pltpu.make_async_copy(src.at[pl.ds(256 * t, 16), :], edge.at[a, t], edge_sem.at[a, t])
             copy.start()
@@ -159,35 +141,25 @@
         copy.start()
         loads.append(copy)
 
-    for copy in edges:
-        copy.wait()
+    barrier = pltpu.get_barrier_semaphore()
+    for who in near:
+        pl.semaphore_signal(barrier, 1, device_id=who, device_id_type=MESH)
+    for who, later in along:
+        @pl.when(later >= 0)
+        def _(who=who):
+            pl.semaphore_signal(barrier, 1, device_id=who, device_id_type=MESH)
+
     row16 = lax.broadcasted_iota(jnp.int32, (16, 1024), 0)
     head16 = lax.broadcasted_iota(jnp.int32, (16, 1024), 1) // 64
-    for a in range(3):
+    my_near = y * 4 + x
+    my_along = z * 2 + core
+
+    def pick_edge(a):
         for t in range(FAR):
             block = edge[a, t].astype(F32)
-            if a == 0:
-                block = block * 0.125
             picked = jnp.sum(jnp.where(row16 == head16, block, 0.0), axis=0, keepdims=True)
             for p in range(PAIRS):
                 far_stage[a, pl.ds(2 * p + t, 1), :] = picked[:, 128 * p : 128 * p + 128]
-    fq_send[...] = far_stage[0].astype(BF16)
-    kv_send[0:16, :] = far_stage[1].astype(BF16)
-    kv_send[16:32, :] = far_stage[2].astype(BF16)
-    my_near = core * 8 + inner
-    my_along = y_lo * 8 + z
-    fq_recv[my_near] = fq_send[...]
-    kv_recv[my_along] = kv_send[...]
-
-    wait_some(barrier, lower_near + lower_along)
-    for who, its in near:
-        @pl.when(its < mine)
-        def _(who=who):
-            pl.semaphore_signal(near_sem, 1, device_id=who, device_id_type=MESH)
-    for who, its in along:
-        @pl.when(its < mine)
-        def _(who=who):
-            pl.semaphore_signal(along_sem, 1, device_id=who, device_id_type=MESH)
 
     def kv_copy(who):
         return pltpu.make_async_remote_copy(
@@ -195,16 +167,34 @@
             device_id=who, device_id_type=MESH,
         )
 
-    for who, its in along:
-        @pl.when(its < mine)
-        def _(who=who):
-            kv_copy(who).start()
-
-    for copy in loads:
+    def fq_copy(who):
+        return pltpu.make_async_remote_copy(
+            src_ref=fq_send, dst_ref=fq_recv.at[my_near], send_sem=fq_ssem, recv_sem=fq_rsem,
+            device_id=who, device_id_type=MESH,
+        )
+
+    def mid_copy(who):
+        return pltpu.make_async_remote_copy(
+            src_ref=mid_send.at[who[1]], dst_ref=mid_recv.at[inner], send_sem=mid_ssem, recv_sem=mid_rsem,
+            device_id=who, device_id_type=MESH,
+        )
+
+    for copy in edges[:4]:
         copy.wait()
+    pick_edge(1)
+    pick_edge(2)
+    kv_send[0:16, :] = far_stage[1].astype(BF16)
+    kv_send[16:32, :] = far_stage[2].astype(BF16)
+    kv_recv[my_along] = kv_send[...]
+    for copy in edges[4:]:
+        copy.wait()
+    pick_edge(0)
+    fq_send[...] = (far_stage[0] * 0.125).astype(BF16)
+    fq_recv[my_near] = fq_send[...]
+
     second = lane_is_second((MID, 128))
 
-    def select_pair(p):
+    def pick(p, carry):
         first_row = (2 * p) % 8
         columns = pl.ds(pl.multiple_of(p * 128, 128), 128)
         for a, ref in enumerate((q_ref, k_ref, v_ref)):
@@ -216,32 +206,36 @@
             one = stage[a, pl.ds(first_row, MID, stride=8), :]
             two = stage[a, pl.ds(first_row + 1, MID, stride=8), :]
             mid_send[p, pl.ds(MID * a, MID), :] = jnp.where(second, two, one).astype(BF16)
-
-    def pick(p, carry):
-        select_pair(p)
         return carry
 
-    lax.fori_loop(0, PAIRS, pick, 0)
-    mid_recv[inner] = mid_send[inner]
-
-    def send_near():
-        wait_some(near_sem, 15 - lower_near)
-        for dx, dy in INNER_STEPS:
-            p = ((x + dx) % 4) * 2 + (y_hi + dy) % 2
-            pltpu.make_async_remote_copy(
-                src_ref=mid_send.at[p], dst_ref=mid_recv.at[inner], send_sem=mid_ssem, recv_sem=mid_rsem,
-                device_id=(outer, p), device_id_type=MESH,
-            ).start()
-        for who, _ in near:
-            pltpu.make_async_remote_copy(
-                src_ref=fq_send, dst_ref=fq_recv.at[my_near], send_sem=fq_ssem, recv_sem=fq_rsem,
-                device_id=who, device_id_type=MESH,
-            ).start()
+
+    def pick_all():
+        for copy in loads:
+            copy.wait()
+        lax.fori_loop(0, PAIRS, pick, 0)
+        mid_recv[inner] = mid_send[inner]
+
+    def meet():
+        pl.semaphore_wait(barrier, 15 + early_along)
+        for who, later in along:
+            @pl.when(later <= 0)
+            def _(who=who):
+                kv_copy(who).start()
+        for who, later in along:
+            @pl.when(later < 0)
+            def _(who=who):
+                pl.semaphore_signal(along_sem, 1, device_id=who, device_id_type=MESH)
+        for who in near:
+            fq_copy(who).start()
+
+    def send_mid():
+        for who in near[:7]:
+            mid_copy(who).start()
 
     def send_along():
-        wait_some(along_sem, 15 - lower_along)
-        for who, its in along:
-            @pl.when(its > mine)
+        wait_some(along_sem, 15 - early_along)
+        for who, later in along:
+            @pl.when(later > 0)
             def _(who=who):
                 kv_copy(who).start()
 
@@ -250,18 +244,17 @@
         pltpu.make_async_copy(got, got, mid_rsem).wait()
         keys = mid_recv[:, MID : 2 * MID, :].reshape(ROWS, 128)
         block = value_block(mid_recv[:, 2 * MID :, :].reshape(ROWS, 128))
-        for half in range(4):
-            q = mid_recv[2 * half : 2 * half + 2, 0:MID, :].reshape(128, 128)
+        for n in range(4):
+            q = mid_recv[2 * n : 2 * n + 2, 0:MID, :].reshape(2 * MID, 128)
             att, lse = finish(scores_of(q, keys), block)
             for s in range(2):
                 rows = slice(MID * s, MID * s + MID)
-                back_send[2 * half + s, 0:MID, :] = att[rows].astype(BF16)
-                back_send[2 * half + s, MID:BACK, :] = pack_lse(lse[rows], 4, 16)
-        for dx, dy in INNER_STEPS:
-            p = ((x + dx) % 4) * 2 + (y_hi + dy) % 2
+                back_send[2 * n + s, 0:MID, :] = att[rows].astype(BF16)
+                back_send[2 * n + s, MID:BACK, :] = pack_lse(lse[rows], 4, 16)
+        for who in near[:7]:
             pltpu.make_async_remote_copy(
-                src_ref=back_send.at[p], dst_ref=back_recv.at[inner], send_sem=back_ssem, recv_sem=back_rsem,
-                device_id=(outer, p), device_id_type=MESH,
+                src_ref=back_send.at[who[1]], dst_ref=back_recv.at[inner], send_sem=back_ssem, recv_sem=back_rsem,
+                device_id=who, device_id_type=MESH,
             ).start()
         back_recv[inner] = back_send[inner]
 
@@ -287,10 +280,11 @@
         for s in range(RG):
             far_send[s, 0:16, :] = far_att[16 * s : 16 * s + 16, :].astype(BF16)
             far_send[s, 16:32, :] = pack_lse(far_lse[16 * s : 16 * s + 16, :], 1, 16)
-        for (o, i), _ in near:
+        for who in near:
+            its_y = who[1] % 2 * 2 + who[0] // 16
             pltpu.make_async_remote_copy(
-                src_ref=far_send.at[(o % 2) * 8 + i], dst_ref=far_recv.at[my_near],
-                send_sem=far_ssem, recv_sem=far_rsem, device_id=(o, i), device_id_type=MESH,
+                src_ref=far_send.at[its_y * 4 + who[1] // 2], dst_ref=far_recv.at[my_near],
+                send_sem=far_ssem, recv_sem=far_rsem, device_id=who, device_id_type=MESH,
             ).start()
         far_recv[my_near] = far_send[my_near]
 
@@ -309,36 +303,30 @@
         two = lse_pair[pl.ds(first_row + 1, MID, stride=8), :]
         lse_ref[p] = jnp.where(second, two, one)
 
-    hops = mine // 256
-    at_near = jnp.where(hops >= 6, 0, jnp.where(hops >= 3, 1, 2))
-    at_along = at_near + 1
-    at_mid = at_near + 3
-    at_far = at_near + 5
+    near_hops = x - 2 * (x // 3) + y - 2 * (y // 3)
+    opens = jnp.where(near_hops >= 3, 0, 3 - near_hops)
+    events = (
+        (opens, meet),
+        (0, pick_all),
+        (jnp.maximum(opens, 1), send_mid),
+        (jnp.where(z < 4, 8 - wave - near_hops // 2, 1), send_along),
+        (9 - near_hops // 2, far),
+        (9 - near_hops // 2, middle),
+    )
 
     def step(t, carry):
-        @pl.when(t == at_near)
+        for at, event in events:
+            @pl.when(t == at)
+            def _(event=event):
+                event()
+
+        @pl.when(jnp.logical_and(t > 0, t <= PAIRS))
         def _():
-            send_near()
-
-        @pl.when(t == at_along)
-        def _():
-            send_along()
-
-        @pl.when(t == at_mid)
-        def _():
-            middle()
-
-        @pl.when(t == at_far)
-        def _():
-            far()
-
-        @pl.when(t < PAIRS)
-        def _():
-            first_level(t)
+            first_level(t - 1)
 
         return carry
 
-    lax.fori_loop(0, PAIRS + 1, step, 0)
+    lax.fori_loop(0, PAIRS + 2, step, 0)
 
     got = back_recv.at[pl.ds(0, INNER - 1)]
     pltpu.make_async_copy(got, got, back_rsem).wait()
@@ -393,13 +381,25 @@
     pltpu.make_async_copy(sent, sent, far_ssem).wait()
 
 
+def store(merged_ref, out_hbm, sem):
+    rows = ROWS // STORES
+    copies = []
+    for n in range(STORES):
+        part = pl.ds(rows * n, rows)
+        copies.append(pltpu.make_async_copy(merged_ref.at[part, :], out_hbm.at[part, :], sem.at[n]))
+    for copy in copies:
+        copy.start()
+    for copy in copies:
+        copy.wait()
+
+
 def on_device(queries, keys, values):
     dma = pltpu.SemaphoreType.DMA
     vmem = pltpu.VMEM
-    return pl.pallas_call(
+    merged = pl.pallas_call(
         kernel,
-        out_shape=jax.ShapeDtypeStruct((ROWS, 1024), BF16),
-        in_specs=[pl.BlockSpec(memory_space=pl.ANY)] * 3,
+        out_shape=pltpu.VMEM((ROWS, 1024), BF16),
+        in_specs=[pl.BlockSpec(memory_space=pltpu.HBM)] * 3,
         out_specs=pl.BlockSpec(memory_space=pltpu.VMEM),
         scratch_shapes=[
             vmem((ROWS, 1024), BF16), vmem((ROWS, 1024), BF16), vmem((ROWS, 1024), BF16),
@@ -410,14 +410,21 @@
             vmem((32, 128), BF16), vmem((GG, 32, 128), BF16), dma, dma,
             vmem((16, 128), BF16), vmem((RG, 16, 128), BF16), dma, dma,
             vmem((RG, 32, 128), BF16), vmem((RG, 32, 128), BF16), dma, dma,
-            pltpu.SemaphoreType.REGULAR, pltpu.SemaphoreType.REGULAR,
+            pltpu.SemaphoreType.REGULAR,
             vmem((PAIRS, ROWS, 128), F32), vmem((ROWS, 128), F32), vmem((PAIRS, MID, 128), F32),
             vmem((256, 128), F32), vmem((256, 128), F32),
         ],
         compiler_params=pltpu.CompilerParams(
             collective_id=0, has_side_effects=True, vmem_limit_bytes=40 * 1024 * 1024
         ),
-    )(queries, keys, values)
+    )(*(pltpu.with_memory_space_constraint(a, pltpu.HBM) for a in (queries, keys, values)))
+    return pl.pallas_call(
+        store,
+        out_shape=pltpu.HBM((ROWS, 1024), BF16),
+        in_specs=[pl.BlockSpec(memory_space=pltpu.VMEM)],
+        out_specs=pl.BlockSpec(memory_space=pltpu.HBM),
+        scratch_shapes=[dma((STORES,))],
+    )(pltpu.with_memory_space_constraint(merged, pltpu.VMEM))
 
 
 def solution(mesh):

time: 31.7 us -> 24.3 us (0.77)
  local copies, waits for them, and re-layouts: 4.65 us -> 0 us
  Pallas kernels: 26.8 us -> 24.2 us
    unnamed x7 -> x0, local copies, waits for them, and re-layouts: 4.65 us -> none
    pallas_call x1 -> x2, Pallas kernels: 26.8 us -> 24.2 us  [the longest x1 23.1 us: on_device(): pl.pallas_call(kernel, out_shape=pltpu.VMEM((ROWS, 1024), BF16), in_specs...]
where the time goes in v2:
time: 24.3 us; the launch traced here: 24.2 us
  Pallas kernels  24.2 us (100%)
    pallas_call x1, Pallas kernels, on_device(): pl.pallas_call(kernel, out_shape=pltpu.VMEM((ROWS, 1024), BF16), in_specs...  23.1 us
    pallas_call x1, Pallas kernels, on_device(): pl.pallas_call(store, out_shape=pltpu.HBM((ROWS, 1024), BF16), in_specs=[...  1.03 us

profile of v2, /device:TPU:1, one launch (start us, length us, event | category | flops | bytes accessed | tf_op | source)
XLA Modules:
  0.0 24.2 jit_solution(9866432129096802416)
XLA Ops:
  0.0 23.1 %shard_map.37.merged_ref = bf16[512,1024]{1,0:T(8,128)(2,1)S(1)} custom-call(bf16[512,1024]{1,0:T(8,128)(2,1)} %q_hbm.1, bf16[512,1024]{1,0:T(8,128)(2,1)} %k_hbm.1, bf16[512,1024]{1,0:T(8,128)(2,1)} %v_hbm.1), custom_call_target="tpu_custom_call" | custom-call | tf_op jit(solution)/shard_map/pallas_call | solution.py:399
  23.1 1.0 %shard_map.38 = bf16[512,1024]{1,0:T(8,128)(2,1)} custom-call(bf16[512,1024]{1,0:T(8,128)(2,1)S(1)} %shard_map.37.merged_ref), custom_call_target="tpu_custom_call" | custom-call | tf_op jit(solution)/shard_map/pallas_call | solution.py:421

commit v3 on v2

--- a/solution.py
+++ b/solution.py
@@ -18,7 +18,6 @@
 GG = 16
 BACK = MID + 16
 LOWEST = -1e30
-STORES = 8
 
 INNER_STEPS = ((2, 2), (1, 2), (3, 2), (2, 0), (0, 2), (1, 0), (3, 0))
 REST_STEPS = ((2, 1), (2, 3), (1, 1), (1, 3), (3, 1), (3, 3), (0, 1), (0, 3))
@@ -88,20 +87,14 @@
     return out
 
 
-def wait_some(sem, count):
-    @pl.when(count > 0)
-    def _():
-        pl.semaphore_wait(sem, count)
-
-
 def kernel(
-    q_hbm, k_hbm, v_hbm, out_ref,
+    q_hbm, k_hbm, v_hbm, merged_ref, two_ref, far_recv,
     q_ref, k_ref, v_ref, edge, load_sem, edge_sem,
     stage, far_stage, mid_send, mid_recv, mid_ssem, mid_rsem,
     back_send, back_recv, back_ssem, back_rsem,
     kv_send, kv_recv, kv_ssem, kv_rsem,
     fq_send, fq_recv, fq_ssem, fq_rsem,
-    far_send, far_recv, far_ssem, far_rsem,
+    far_send, far_ssem, far_rsem,
     along_sem, att_ref, lse_pair, lse_ref, far_att, far_lse,
 ):
     outer = lax.axis_index("outer")
@@ -126,8 +119,15 @@
         for dc in range(2):
             if dz or dc:
                 pz = (z + dz) % 8
-                along.append(((outer_id(y_lo, pz, (core + dc) % 2), inner), jnp.minimum(pz, 4) - wave))
+                along.append(((outer_id(y_lo, pz, (core + dc) % 2), inner), jnp.minimum(pz, 4) - wave, pz))
     early_along = jnp.where(z < 4, 2 * z + 1, 15)
+
+    entry = sum(9 * v - 2 * (v // 2) - 11 * (v // 3) for v in (x, y))
+    opens = jnp.where(entry < 24, 1, 0)
+    at_mid = 7 + opens
+    at_far = at_mid + jnp.where(entry < 5, 1, 0)
+    at_along_early = jnp.where(z < 3, 4 + opens - z, -1)
+    at_along_late = jnp.where(z < 4, at_mid - jnp.where(z == 0, 0, wave) + wave // 3, -1)
 
     edges = []
     for a, src in ((1, k_hbm), (2, v_hbm), (0, q_hbm)):
@@ -144,7 +144,7 @@
     barrier = pltpu.get_barrier_semaphore()
     for who in near:
         pl.semaphore_signal(barrier, 1, device_id=who, device_id_type=MESH)
-    for who, later in along:
+    for who, later, _ in along:
         @pl.when(later >= 0)
         def _(who=who):
             pl.semaphore_signal(barrier, 1, device_id=who, device_id_type=MESH)
@@ -194,7 +194,7 @@
 
     second = lane_is_second((MID, 128))
 
-    def pick(p, carry):
+    def pick(p):
         first_row = (2 * p) % 8
         columns = pl.ds(pl.multiple_of(p * 128, 128), 128)
         for a, ref in enumerate((q_ref, k_ref, v_ref)):
@@ -206,25 +206,34 @@
             one = stage[a, pl.ds(first_row, MID, stride=8), :]
             two = stage[a, pl.ds(first_row + 1, MID, stride=8), :]
             mid_send[p, pl.ds(MID * a, MID), :] = jnp.where(second, two, one).astype(BF16)
-        return carry
 
 
     def pick_all():
         for copy in loads:
             copy.wait()
-        lax.fori_loop(0, PAIRS, pick, 0)
+        for who in near[:7]:
+            pick(who[1])
+
+            @pl.when(opens == 0)
+            def _(who=who):
+                mid_copy(who).start()
+        pick(inner)
         mid_recv[inner] = mid_send[inner]
 
     def meet():
         pl.semaphore_wait(barrier, 15 + early_along)
-        for who, later in along:
-            @pl.when(later <= 0)
+        for who, later, _ in along:
+            @pl.when(later < 0)
             def _(who=who):
                 kv_copy(who).start()
-        for who, later in along:
+        for who, later, _ in along:
             @pl.when(later < 0)
             def _(who=who):
-                pl.semaphore_signal(along_sem, 1, device_id=who, device_id_type=MESH)
+                pl.semaphore_signal(along_sem.at[jnp.where(z < 4, 0, 1)], 1, device_id=who, device_id_type=MESH)
+        for who, later, _ in along:
+            @pl.when(later == 0)
+            def _(who=who):
+                kv_copy(who).start()
         for who in near:
             fq_copy(who).start()
 
@@ -232,10 +241,17 @@
         for who in near[:7]:
             mid_copy(who).start()
 
-    def send_along():
-        wait_some(along_sem, 15 - early_along)
-        for who, later in along:
-            @pl.when(later > 0)
+    def send_along_early():
+        pl.semaphore_wait(along_sem.at[0], 6 - 2 * z)
+        for who, later, pz in along:
+            @pl.when(jnp.logical_and(later > 0, pz < 4))
+            def _(who=who):
+                kv_copy(who).start()
+
+    def send_along_late():
+        pl.semaphore_wait(along_sem.at[1], 8)
+        for who, later, pz in along:
+            @pl.when(jnp.logical_and(later > 0, pz >= 4))
             def _(who=who):
                 kv_copy(who).start()
 
@@ -303,15 +319,14 @@
         two = lse_pair[pl.ds(first_row + 1, MID, stride=8), :]
         lse_ref[p] = jnp.where(second, two, one)
 
-    near_hops = x - 2 * (x // 3) + y - 2 * (y // 3)
-    opens = jnp.where(near_hops >= 3, 0, 3 - near_hops)
     events = (
         (opens, meet),
         (0, pick_all),
-        (jnp.maximum(opens, 1), send_mid),
-        (jnp.where(z < 4, 8 - wave - near_hops // 2, 1), send_along),
-        (9 - near_hops // 2, far),
-        (9 - near_hops // 2, middle),
+        (jnp.where(opens > 0, opens, -1), send_mid),
+        (at_along_early, send_along_early),
+        (at_along_late, send_along_late),
+        (at_mid, middle),
+        (at_far, far),
     )
 
     def step(t, carry):
@@ -330,44 +345,28 @@
 
     got = back_recv.at[pl.ds(0, INNER - 1)]
     pltpu.make_async_copy(got, got, back_rsem).wait()
-    got = far_recv.at[pl.ds(0, RG - 1)]
-    pltpu.make_async_copy(got, got, far_rsem).wait()
-
-    partial_lse = unpack_lse(far_recv[:, 16:32, :].reshape(256, 128), 1, 16)[0]
-    top = partial_lse[0:16]
-    for s in range(1, RG):
-        top = jnp.maximum(top, partial_lse[16 * s : 16 * s + 16])
-    numer = jnp.zeros((16, 128), F32)
-    denom = jnp.zeros((16, 128), F32)
-    for s in range(RG):
-        weight = jnp.exp(partial_lse[16 * s : 16 * s + 16] - top)
-        numer = numer + weight * far_recv[s, 0:16, :].astype(F32)
-        denom = denom + weight
-    far_att[0:16, :] = numer / denom
-    far_lse[0:16, :] = top + jnp.log(denom)
-
     mid_lse = unpack_lse(back_recv[:, MID:BACK, :].reshape(128, 128), 4, 16)
     for p in range(PAIRS):
         first_row = (2 * p) % 8
         one = att_ref[p, pl.ds(first_row, MID, stride=8), :]
         two = att_ref[p, pl.ds(first_row + 1, MID, stride=8), :]
-        att1 = jnp.where(second, two, one)
         lse1 = lse_ref[p]
-        att2 = back_recv[p, 0:MID, :].astype(F32)
         lse2 = jnp.concatenate([mid_lse[g][16 * p : 16 * p + 16] for g in range(4)], axis=0)
-        row = lax.broadcasted_iota(jnp.int32, (MID, 128), 0)
-        att3 = jnp.zeros((MID, 128), F32)
-        lse3 = jnp.full((MID, 128), LOWEST, F32)
+        top = jnp.maximum(lse1, lse2)
+        w1, w2 = jnp.exp(lse1 - top), jnp.exp(lse2 - top)
+        total = w1 + w2
+        merged = (w1 * jnp.where(second, two, one) + w2 * back_recv[p, 0:MID, :].astype(F32)) / total
+        lse = top + jnp.log(total)
         for t in range(FAR):
-            here = row == 32 * t + p // 4
-            att3 = jnp.where(here, far_att[2 * p + t : 2 * p + t + 1, :], att3)
-            lse3 = jnp.where(here, far_lse[2 * p + t : 2 * p + t + 1, :], lse3)
-        top = jnp.maximum(jnp.maximum(lse1, lse2), lse3)
-        w1, w2, w3 = jnp.exp(lse1 - top), jnp.exp(lse2 - top), jnp.exp(lse3 - top)
-        merged = (w1 * att1 + w2 * att2 + w3 * att3) / (w1 + w2 + w3)
+            row = 32 * t + p // 4
+            two_ref[0, 2 * p + t : 2 * p + t + 1, :] = merged[row : row + 1]
+            two_ref[1, 2 * p + t : 2 * p + t + 1, :] = lse[row : row + 1]
         att_ref[p, pl.ds(first_row, MID, stride=8), :] = jnp.where(second, one, merged)
         att_ref[p, pl.ds(first_row + 1, MID, stride=8), :] = jnp.where(second, merged, two)
-        out_ref[:, 128 * p : 128 * p + 128] = att_ref[p].astype(BF16)
+        merged_ref[:, 128 * p : 128 * p + 128] = att_ref[p].astype(BF16)
+
+    got = far_recv.at[pl.ds(0, RG - 1)]
+    pltpu.make_async_copy(got, got, far_rsem).wait()
 
     sent = mid_send.at[pl.ds(0, INNER - 1)]
     pltpu.make_async_copy(sent, sent, mid_ssem).wait()
@@ -381,14 +380,36 @@
     pltpu.make_async_copy(sent, sent, far_ssem).wait()
 
 
-def store(merged_ref, out_hbm, sem):
-    rows = ROWS // STORES
+def merge(merged_ref, two_ref, far_recv, out_hbm, edge, sem):
     copies = []
-    for n in range(STORES):
-        part = pl.ds(rows * n, rows)
-        copies.append(pltpu.make_async_copy(merged_ref.at[part, :], out_hbm.at[part, :], sem.at[n]))
-    for copy in copies:
-        copy.start()
+    for t in range(FAR):
+        rest = pl.ds(256 * t + 16, 240)
+        copies.append(pltpu.make_async_copy(merged_ref.at[rest, :], out_hbm.at[rest, :], sem.at[t]))
+        copies[t].start()
+
+    partial_lse = unpack_lse(far_recv[:, 16:32, :].reshape(256, 128), 1, 16)[0]
+    top = two_ref[1]
+    for s in range(RG):
+        top = jnp.maximum(top, partial_lse[16 * s : 16 * s + 16])
+    weight = jnp.exp(two_ref[1] - top)
+    numer = weight * two_ref[0]
+    denom = weight
+    for s in range(RG):
+        weight = jnp.exp(partial_lse[16 * s : 16 * s + 16] - top)
+        numer = numer + weight * far_recv[s, 0:16, :].astype(F32)
+        denom = denom + weight
+    result = numer / denom
+
+    row = lax.broadcasted_iota(jnp.int32, (16, 128), 0)
+    half = lax.broadcasted_iota(jnp.int32, (16, 128), 1) // 64
+    for t in range(FAR):
+        for p in range(PAIRS):
+            columns = slice(128 * p, 128 * p + 128)
+            old = merged_ref[256 * t : 256 * t + 16, columns].astype(F32)
+            new = jnp.where(row == 2 * p + half, result[2 * p + t : 2 * p + t + 1], old)
+            edge[t, :, columns] = new.astype(BF16)
+        copies.append(pltpu.make_async_copy(edge.at[t], out_hbm.at[pl.ds(256 * t, 16), :], sem.at[FAR + t]))
+        copies[FAR + t].start()
     for copy in copies:
         copy.wait()
 
@@ -396,11 +417,13 @@
 def on_device(queries, keys, values):
     dma = pltpu.SemaphoreType.DMA
     vmem = pltpu.VMEM
-    merged = pl.pallas_call(
+    results = pl.pallas_call(
         kernel,
-        out_shape=pltpu.VMEM((ROWS, 1024), BF16),
+        out_shape=[
+            vmem((ROWS, 1024), BF16), vmem((2, 16, 128), F32), vmem((RG, 32, 128), BF16),
+        ],
         in_specs=[pl.BlockSpec(memory_space=pltpu.HBM)] * 3,
-        out_specs=pl.BlockSpec(memory_space=pltpu.VMEM),
+        out_specs=[pl.BlockSpec(memory_space=pltpu.VMEM)] * 3,
         scratch_shapes=[
             vmem((ROWS, 1024), BF16), vmem((ROWS, 1024), BF16), vmem((ROWS, 1024), BF16),
             vmem((3, FAR, 16, 1024), BF16), dma((3,)), dma((3, FAR)),
@@ -409,8 +432,8 @@
             vmem((INNER, BACK, 128), BF16), vmem((INNER, BACK, 128), BF16), dma, dma,
             vmem((32, 128), BF16), vmem((GG, 32, 128), BF16), dma, dma,
             vmem((16, 128), BF16), vmem((RG, 16, 128), BF16), dma, dma,
-            vmem((RG, 32, 128), BF16), vmem((RG, 32, 128), BF16), dma, dma,
-            pltpu.SemaphoreType.REGULAR,
+            vmem((RG, 32, 128), BF16), dma, dma,
+            pltpu.SemaphoreType.REGULAR((2,)),
             vmem((PAIRS, ROWS, 128), F32), vmem((ROWS, 128), F32), vmem((PAIRS, MID, 128), F32),
             vmem((256, 128), F32), vmem((256, 128), F32),
         ],
@@ -419,12 +442,15 @@
         ),
     )(*(pltpu.with_memory_space_constraint(a, pltpu.HBM) for a in (queries, keys, values)))
     return pl.pallas_call(
-        store,
+        merge,
         out_shape=pltpu.HBM((ROWS, 1024), BF16),
-        in_specs=[pl.BlockSpec(memory_space=pltpu.VMEM)],
+        in_specs=[pl.BlockSpec(memory_space=pltpu.VMEM)] * 3,
         out_specs=pl.BlockSpec(memory_space=pltpu.HBM),
-        scratch_shapes=[dma((STORES,))],
-    )(pltpu.with_memory_space_constraint(merged, pltpu.VMEM))
+        scratch_shapes=[
+            vmem((FAR, 16, 1024), BF16), dma((2 * FAR,)),
+        ],
+        compiler_params=pltpu.CompilerParams(vmem_limit_bytes=16 * 1024 * 1024),
+    )(*(pltpu.with_memory_space_constraint(a, pltpu.VMEM) for a in results))
 
 
 def solution(mesh):

time: 24.3 us -> 22.1 us (0.909)
  Pallas kernels: 24.2 us -> 22 us
    pallas_call x2, Pallas kernels: 24.2 us -> 22 us  [the longest x1 21 us: on_device(): pl.pallas_call(kernel, out_shape=[vmem((ROWS, 1024), BF16), vmem((2, 16,...]
where the time goes in v3:
time: 22.1 us; the launch traced here: 22 us
  Pallas kernels  22 us (100%)
    pallas_call x1, Pallas kernels, on_device(): pl.pallas_call(kernel, out_shape=[vmem((ROWS, 1024), BF16), vmem((2, 16,...  21 us
    pallas_call x1, Pallas kernels, on_device(): pl.pallas_call(merge, out_shape=pltpu.HBM((ROWS, 1024), BF16), in_specs=[...  0.99 us

profile of v3, /device:TPU:1, one launch (start us, length us, event | category | flops | bytes accessed | tf_op | source)
XLA Modules:
  0.0 22.0 jit_solution(15236500052999027273)
XLA Ops:
  0.0 21.0 %shard_map.37 = (bf16[512,1024]{1,0:T(8,128)(2,1)S(1)}, f32[2,16,128]{2,1,0:T(8,128)S(1)}, bf16[16,32,128]{2,1,0:T(8,128)(2,1)S(1)}) custom-call(bf16[512,1024]{1,0:T(8,128)(2,1)} %q_hbm.1, bf16[512,1024]{1,0:T(8,128)(2,1)} %k_hbm.1, bf16[512,1024]{1,0:T(8,128)(2,1)} %v_hbm.1), custom_call_target="tpu_custom_call" | custom-call | tf_op jit(solution)/shard_map/pallas_call | solution.py:420
  21.0 1.0 %shard_map.38 = bf16[512,1024]{1,0:T(8,128)(2,1)} custom-call(bf16[512,1024]{1,0:T(8,128)(2,1)S(1)} %get-tuple-element.8.merged_ref, f32[2,16,128]{2,1,0:T(8,128)S(1)} %get-tuple-element.9.two_ref, bf16[16,32,128]{2,1,0:T(8,128)(2,1)S(1)} %get-tuple-element.10.far_recv), custom_call_target="tpu_custom_call" | custom-call | tf_op jit(solution)/shard_map/pallas_call | solution.py:444

commit v4 on v3

--- a/solution.py
+++ b/solution.py
@@ -21,7 +21,6 @@
 
 INNER_STEPS = ((2, 2), (1, 2), (3, 2), (2, 0), (0, 2), (1, 0), (3, 0))
 REST_STEPS = ((2, 1), (2, 3), (1, 1), (1, 3), (3, 1), (3, 3), (0, 1), (0, 3))
-Z_STEPS = (4, 3, 5, 2, 6, 1, 7, 0)
 
 
 def lane_is_second(shape):
@@ -115,19 +114,27 @@
         px, py = (x + dx) % 4, (y + dy) % 4
         near.append((outer_id(py % 2, z, core), px * 2 + py // 2))
     wave = jnp.minimum(z, 4)
-    for dz in Z_STEPS:
-        for dc in range(2):
-            if dz or dc:
-                pz = (z + dz) % 8
-                along.append(((outer_id(y_lo, pz, (core + dc) % 2), inner), jnp.minimum(pz, 4) - wave, pz))
+    for pz in range(8):
+        for pc in range(2):
+            here = jnp.logical_and(z == pz, core == pc)
+            later = jnp.where(here, 9, min(pz, 4) - wave)
+            along.append(((outer_id(y_lo, pz, pc), inner), later, pz))
     early_along = jnp.where(z < 4, 2 * z + 1, 15)
 
     entry = sum(9 * v - 2 * (v // 2) - 11 * (v // 3) for v in (x, y))
-    opens = jnp.where(entry < 24, 1, 0)
-    at_mid = 7 + opens
-    at_far = at_mid + jnp.where(entry < 5, 1, 0)
+    opens = jnp.where(entry < 20, 1, 0)
+    at_mid = 6 + opens + jnp.where(entry < 5, 1, 0)
+    at_far = at_mid
     at_along_early = jnp.where(z < 3, 4 + opens - z, -1)
-    at_along_late = jnp.where(z < 4, at_mid - jnp.where(z == 0, 0, wave) + wave // 3, -1)
+    at_along_late = jnp.where(z < 4, at_mid - wave + wave // 3, -1)
+
+    barrier = pltpu.get_barrier_semaphore()
+    for who in near:
+        pl.semaphore_signal(barrier, 1, device_id=who, device_id_type=MESH)
+    for who, later, _ in along:
+        @pl.when(jnp.logical_and(later >= 0, later < 9))
+        def _(who=who):
+            pl.semaphore_signal(barrier, 1, device_id=who, device_id_type=MESH)
 
     edges = []
     for a, src in ((1, k_hbm), (2, v_hbm), (0, q_hbm)):
@@ -141,14 +148,6 @@
         copy.start()
         loads.append(copy)
 
-    barrier = pltpu.get_barrier_semaphore()
-    for who in near:
-        pl.semaphore_signal(barrier, 1, device_id=who, device_id_type=MESH)
-    for who, later, _ in along:
-        @pl.when(later >= 0)
-        def _(who=who):
-            pl.semaphore_signal(barrier, 1, device_id=who, device_id_type=MESH)
-
     row16 = lax.broadcasted_iota(jnp.int32, (16, 1024), 0)
     head16 = lax.broadcasted_iota(jnp.int32, (16, 1024), 1) // 64
     my_near = y * 4 + x
@@ -186,12 +185,6 @@
     kv_send[0:16, :] = far_stage[1].astype(BF16)
     kv_send[16:32, :] = far_stage[2].astype(BF16)
     kv_recv[my_along] = kv_send[...]
-    for copy in edges[4:]:
-        copy.wait()
-    pick_edge(0)
-    fq_send[...] = (far_stage[0] * 0.125).astype(BF16)
-    fq_recv[my_near] = fq_send[...]
-
     second = lane_is_second((MID, 128))
 
     def pick(p):
@@ -234,26 +227,34 @@
             @pl.when(later == 0)
             def _(who=who):
                 kv_copy(who).start()
+
+    def send_mid():
+        @pl.when(opens > 0)
+        def _():
+            for who in near[:7]:
+                mid_copy(who).start()
+
+        for copy in edges[4:]:
+            copy.wait()
+        pick_edge(0)
+        fq_send[...] = (far_stage[0] * 0.125).astype(BF16)
+        fq_recv[my_near] = fq_send[...]
         for who in near:
             fq_copy(who).start()
 
-    def send_mid():
-        for who in near[:7]:
-            mid_copy(who).start()
+    def send_along(half):
+        for who, later, pz in along[8 * half : 8 * half + 8]:
+            @pl.when(jnp.logical_and(later > 0, later < 9))
+            def _(who=who):
+                kv_copy(who).start()
 
     def send_along_early():
         pl.semaphore_wait(along_sem.at[0], 6 - 2 * z)
-        for who, later, pz in along:
-            @pl.when(jnp.logical_and(later > 0, pz < 4))
-            def _(who=who):
-                kv_copy(who).start()
+        send_along(0)
 
     def send_along_late():
         pl.semaphore_wait(along_sem.at[1], 8)
-        for who, later, pz in along:
-            @pl.when(jnp.logical_and(later > 0, pz >= 4))
-            def _(who=who):
-                kv_copy(who).start()
+        send_along(1)
 
     def middle():
         got = mid_recv.at[pl.ds(0, INNER - 1)]
@@ -275,12 +276,12 @@
         back_recv[inner] = back_send[inner]
 
     def far():
+        got = fq_recv.at[pl.ds(0, RG - 1)]
+        pltpu.make_async_copy(got, got, fq_rsem).wait()
+        stage[1, 0:256, :] = fq_recv[...].reshape(256, 128).astype(F32)
         got = kv_recv.at[pl.ds(0, GG - 1)]
         pltpu.make_async_copy(got, got, kv_rsem).wait()
-        got = fq_recv.at[pl.ds(0, RG - 1)]
-        pltpu.make_async_copy(got, got, fq_rsem).wait()
         stage[0] = kv_recv[...].reshape(ROWS, 128).astype(F32)
-        stage[1, 0:256, :] = fq_recv[...].reshape(256, 128).astype(F32)
         scores, blocks = [], []
         for p in range(PAIRS):
             q = jnp.concatenate([stage[1, pl.ds(2 * p + t, RG, stride=16), :] for t in range(FAR)], axis=0)
@@ -322,7 +323,7 @@
     events = (
         (opens, meet),
         (0, pick_all),
-        (jnp.where(opens > 0, opens, -1), send_mid),
+        (opens, send_mid),
         (at_along_early, send_along_early),
         (at_along_late, send_along_late),
         (at_mid, middle),
@@ -365,9 +366,6 @@
         att_ref[p, pl.ds(first_row + 1, MID, stride=8), :] = jnp.where(second, merged, two)
         merged_ref[:, 128 * p : 128 * p + 128] = att_ref[p].astype(BF16)
 
-    got = far_recv.at[pl.ds(0, RG - 1)]
-    pltpu.make_async_copy(got, got, far_rsem).wait()
-
     sent = mid_send.at[pl.ds(0, INNER - 1)]
     pltpu.make_async_copy(sent, sent, mid_ssem).wait()
     sent = back_send.at[pl.ds(0, INNER - 1)]
@@ -378,6 +376,9 @@
     pltpu.make_async_copy(sent, sent, fq_ssem).wait()
     sent = far_send.at[pl.ds(0, RG - 1)]
     pltpu.make_async_copy(sent, sent, far_ssem).wait()
+
+    got = far_recv.at[pl.ds(0, RG - 1)]
+    pltpu.make_async_copy(got, got, far_rsem).wait()
 
 
 def merge(merged_ref, two_ref, far_recv, out_hbm, edge, sem):

time: 22.1 us -> 21.6 us (0.977)
  Pallas kernels: 22 us -> 21.5 us
    pallas_call x1, Pallas kernels: 21 us -> 20.5 us  [on_device(): pl.pallas_call(kernel, out_shape=[vmem((ROWS, 1024), BF16), vmem((2, 16,...]
where the time goes in v4:
time: 21.6 us; the launch traced here: 21.5 us
  Pallas kernels  21.5 us (100%)
    pallas_call x1, Pallas kernels, on_device(): pl.pallas_call(kernel, out_shape=[vmem((ROWS, 1024), BF16), vmem((2, 16,...  20.5 us
    pallas_call x1, Pallas kernels, on_device(): pl.pallas_call(merge, out_shape=pltpu.HBM((ROWS, 1024), BF16), in_specs=[...  0.99 us

profile of v4, /device:TPU:1, one launch (start us, length us, event | category | flops | bytes accessed | tf_op | source)
XLA Modules:
  0.0 21.5 jit_solution(14741240632597373480)
XLA Ops:
  0.0 20.5 %shard_map.37 = (bf16[512,1024]{1,0:T(8,128)(2,1)S(1)}, f32[2,16,128]{2,1,0:T(8,128)S(1)}, bf16[16,32,128]{2,1,0:T(8,128)(2,1)S(1)}) custom-call(bf16[512,1024]{1,0:T(8,128)(2,1)} %q_hbm.1, bf16[512,1024]{1,0:T(8,128)(2,1)} %k_hbm.1, bf16[512,1024]{1,0:T(8,128)(2,1)} %v_hbm.1), custom_call_target="tpu_custom_call" | custom-call | tf_op jit(solution)/shard_map/pallas_call | solution.py:421
  20.5 1.0 %shard_map.38 = bf16[512,1024]{1,0:T(8,128)(2,1)} custom-call(bf16[512,1024]{1,0:T(8,128)(2,1)S(1)} %get-tuple-element.8.merged_ref, f32[2,16,128]{2,1,0:T(8,128)S(1)} %get-tuple-element.9.two_ref, bf16[16,32,128]{2,1,0:T(8,128)(2,1)S(1)} %get-tuple-element.10.far_recv), custom_call_target="tpu_custom_call" | custom-call | tf_op jit(solution)/shard_map/pallas_call | solution.py:445

commit v5 on v4

--- a/solution.py
+++ b/solution.py
@@ -16,7 +16,6 @@
 INNER = 8
 RG = 16
 GG = 16
-BACK = MID + 16
 LOWEST = -1e30
 
 INNER_STEPS = ((2, 2), (1, 2), (3, 2), (2, 0), (0, 2), (1, 0), (3, 0))
@@ -64,33 +63,33 @@
     return high, mid, (rest - mid.astype(F32)).astype(BF16)
 
 
-def pack_lse(lse, groups, width):
-    high, mid, low = (p.astype(F32) for p in parts_of(lse))
-    lane = lax.broadcasted_iota(jnp.int32, (16, 128), 1) % 64
-    out = jnp.zeros((16, 128), F32)
-    for g in range(groups):
-        rows = slice(16 * g, 16 * g + 16)
-        for t, part in enumerate((high, mid, low)):
-            out = jnp.where(lane == g * width + t, part[rows], out)
-    return out.astype(BF16)
-
-
-def unpack_lse(packed, groups, width):
-    row = lax.broadcasted_iota(jnp.int32, (128, 128), 0)
-    lane = lax.broadcasted_iota(jnp.int32, (128, 128), 1)
-    out = []
-    for g in range(groups):
-        at = row % 64 - g * width
-        take = jnp.logical_and(jnp.logical_and(at >= 0, at < 3), row // 64 == lane // 64)
-        out.append(jnp.dot(packed, jnp.where(take, 1.0, 0.0).astype(BF16), preferred_element_type=F32))
-    return out
+def diagonal(rows, parts, width):
+    row = lax.broadcasted_iota(jnp.int32, (rows, 128), 0)
+    lane = lax.broadcasted_iota(jnp.int32, (rows, 128), 1) % 64
+    return [lane == row + t * width for t in range(parts)]
+
+
+def lse_rows(lse, wide):
+    n = lse.shape[0]
+    masks = diagonal(n, 3, 0 if wide else 16)
+    picked = [
+        jnp.sum(jnp.where(mask, part.astype(F32), 0.0), axis=0, keepdims=True)
+        for mask, part in zip(masks, parts_of(lse), strict=True)
+    ]
+    return jnp.concatenate(picked, axis=1) if wide else picked[0] + picked[1] + picked[2]
+
+
+def half_sums(width):
+    row = lax.broadcasted_iota(jnp.int32, (width, 128), 0)
+    lane = lax.broadcasted_iota(jnp.int32, (width, 128), 1)
+    return jnp.where(row % 128 // 64 == lane // 64, 1.0, 0.0).astype(BF16)
 
 
 def kernel(
-    q_hbm, k_hbm, v_hbm, merged_ref, two_ref, far_recv,
+    q_hbm, k_hbm, v_hbm, merged_ref, two_ref, far_recv, far_lse_recv,
     q_ref, k_ref, v_ref, edge, load_sem, edge_sem,
     stage, far_stage, mid_send, mid_recv, mid_ssem, mid_rsem,
-    back_send, back_recv, back_ssem, back_rsem,
+    back_send, back_recv, back_ssem, back_rsem, back_lse_send, back_lse_recv, far_lse_send, lse_ssem, lse_rsem,
     kv_send, kv_recv, kv_ssem, kv_rsem,
     fq_send, fq_recv, fq_ssem, fq_rsem,
     far_send, far_ssem, far_rsem,
@@ -266,14 +265,19 @@
             att, lse = finish(scores_of(q, keys), block)
             for s in range(2):
                 rows = slice(MID * s, MID * s + MID)
-                back_send[2 * n + s, 0:MID, :] = att[rows].astype(BF16)
-                back_send[2 * n + s, MID:BACK, :] = pack_lse(lse[rows], 4, 16)
+                back_send[2 * n + s] = att[rows].astype(BF16)
+                back_lse_send[2 * n + s] = lse_rows(lse[rows], True)
         for who in near[:7]:
             pltpu.make_async_remote_copy(
                 src_ref=back_send.at[who[1]], dst_ref=back_recv.at[inner], send_sem=back_ssem, recv_sem=back_rsem,
                 device_id=who, device_id_type=MESH,
             ).start()
+            pltpu.make_async_remote_copy(
+                src_ref=back_lse_send.at[who[1]], dst_ref=back_lse_recv.at[inner],
+                send_sem=lse_ssem.at[0], recv_sem=lse_rsem.at[0], device_id=who, device_id_type=MESH,
+            ).start()
         back_recv[inner] = back_send[inner]
+        back_lse_recv[inner] = back_lse_send[inner]
 
     def far():
         got = fq_recv.at[pl.ds(0, RG - 1)]
@@ -295,15 +299,20 @@
                 far_att[pl.ds(2 * p + t, RG, stride=16), :] = att[RG * t : RG * t + RG]
                 far_lse[pl.ds(2 * p + t, RG, stride=16), :] = lse[RG * t : RG * t + RG]
         for s in range(RG):
-            far_send[s, 0:16, :] = far_att[16 * s : 16 * s + 16, :].astype(BF16)
-            far_send[s, 16:32, :] = pack_lse(far_lse[16 * s : 16 * s + 16, :], 1, 16)
+            far_send[s] = far_att[16 * s : 16 * s + 16, :].astype(BF16)
+            far_lse_send[s] = lse_rows(far_lse[16 * s : 16 * s + 16, :], False)
         for who in near:
             its_y = who[1] % 2 * 2 + who[0] // 16
             pltpu.make_async_remote_copy(
                 src_ref=far_send.at[its_y * 4 + who[1] // 2], dst_ref=far_recv.at[my_near],
                 send_sem=far_ssem, recv_sem=far_rsem, device_id=who, device_id_type=MESH,
             ).start()
+            pltpu.make_async_remote_copy(
+                src_ref=far_lse_send.at[its_y * 4 + who[1] // 2], dst_ref=far_lse_recv.at[my_near],
+                send_sem=lse_ssem.at[1], recv_sem=lse_rsem.at[1], device_id=who, device_id_type=MESH,
+            ).start()
         far_recv[my_near] = far_send[my_near]
+        far_lse_recv[my_near] = far_lse_send[my_near]
 
     def first_level(p):
         columns = pl.ds(pl.multiple_of(p * 128, 128), 128)
@@ -346,17 +355,21 @@
 
     got = back_recv.at[pl.ds(0, INNER - 1)]
     pltpu.make_async_copy(got, got, back_rsem).wait()
-    mid_lse = unpack_lse(back_recv[:, MID:BACK, :].reshape(128, 128), 4, 16)
+    got = back_lse_recv.at[pl.ds(0, INNER - 1)]
+    pltpu.make_async_copy(got, got, lse_rsem.at[0]).wait()
+    mask = jnp.concatenate(diagonal(MID, 3, 0), axis=1)
+    spread = half_sums(3 * 128)
     for p in range(PAIRS):
         first_row = (2 * p) % 8
         one = att_ref[p, pl.ds(first_row, MID, stride=8), :]
         two = att_ref[p, pl.ds(first_row + 1, MID, stride=8), :]
         lse1 = lse_ref[p]
-        lse2 = jnp.concatenate([mid_lse[g][16 * p : 16 * p + 16] for g in range(4)], axis=0)
+        lse2 = jnp.where(mask, back_lse_recv[p], 0.0).astype(BF16)
+        lse2 = jnp.dot(lse2, spread, preferred_element_type=F32)
         top = jnp.maximum(lse1, lse2)
         w1, w2 = jnp.exp(lse1 - top), jnp.exp(lse2 - top)
         total = w1 + w2
-        merged = (w1 * jnp.where(second, two, one) + w2 * back_recv[p, 0:MID, :].astype(F32)) / total
+        merged = (w1 * jnp.where(second, two, one) + w2 * back_recv[p].astype(F32)) / total
         lse = top + jnp.log(total)
         for t in range(FAR):
             row = 32 * t + p // 4
@@ -376,19 +389,28 @@
     pltpu.make_async_copy(sent, sent, fq_ssem).wait()
     sent = far_send.at[pl.ds(0, RG - 1)]
     pltpu.make_async_copy(sent, sent, far_ssem).wait()
+    sent = back_lse_send.at[pl.ds(0, INNER - 1)]
+    pltpu.make_async_copy(sent, sent, lse_ssem.at[0]).wait()
+    sent = far_lse_send.at[pl.ds(0, RG - 1)]
+    pltpu.make_async_copy(sent, sent, lse_ssem.at[1]).wait()
 
     got = far_recv.at[pl.ds(0, RG - 1)]
     pltpu.make_async_copy(got, got, far_rsem).wait()
-
-
-def merge(merged_ref, two_ref, far_recv, out_hbm, edge, sem):
+    got = far_lse_recv.at[pl.ds(0, RG - 1)]
+    pltpu.make_async_copy(got, got, lse_rsem.at[1]).wait()
+
+
+def merge(merged_ref, two_ref, far_recv, far_lse_recv, out_hbm, edge, sem):
     copies = []
     for t in range(FAR):
         rest = pl.ds(256 * t + 16, 240)
         copies.append(pltpu.make_async_copy(merged_ref.at[rest, :], out_hbm.at[rest, :], sem.at[t]))
         copies[t].start()
 
-    partial_lse = unpack_lse(far_recv[:, 16:32, :].reshape(256, 128), 1, 16)[0]
+    mask = diagonal(16, 3, 16)
+    mask = jnp.logical_or(jnp.logical_or(mask[0], mask[1]), mask[2])
+    partial_lse = jnp.concatenate([jnp.where(mask, far_lse_recv[s], 0.0) for s in range(RG)], axis=0).astype(BF16)
+    partial_lse = jnp.dot(partial_lse, half_sums(128), preferred_element_type=F32)
     top = two_ref[1]
     for s in range(RG):
         top = jnp.maximum(top, partial_lse[16 * s : 16 * s + 16])
@@ -397,7 +419,7 @@
     denom = weight
     for s in range(RG):
         weight = jnp.exp(partial_lse[16 * s : 16 * s + 16] - top)
-        numer = numer + weight * far_recv[s, 0:16, :].astype(F32)
+        numer = numer + weight * far_recv[s].astype(F32)
         denom = denom + weight
     result = numer / denom
 
@@ -421,19 +443,20 @@
     results = pl.pallas_call(
         kernel,
         out_shape=[
-            vmem((ROWS, 1024), BF16), vmem((2, 16, 128), F32), vmem((RG, 32, 128), BF16),
+            vmem((ROWS, 1024), BF16), vmem((2, 16, 128), F32), vmem((RG, 16, 128), BF16), vmem((RG, 1, 128), F32),
         ],
         in_specs=[pl.BlockSpec(memory_space=pltpu.HBM)] * 3,
-        out_specs=[pl.BlockSpec(memory_space=pltpu.VMEM)] * 3,
+        out_specs=[pl.BlockSpec(memory_space=pltpu.VMEM)] * 4,
         scratch_shapes=[
             vmem((ROWS, 1024), BF16), vmem((ROWS, 1024), BF16), vmem((ROWS, 1024), BF16),
             vmem((3, FAR, 16, 1024), BF16), dma((3,)), dma((3, FAR)),
             vmem((3, ROWS, 128), F32), vmem((3, 16, 128), F32),
             vmem((INNER, 3 * MID, 128), BF16), vmem((INNER, 3 * MID, 128), BF16), dma, dma,
-            vmem((INNER, BACK, 128), BF16), vmem((INNER, BACK, 128), BF16), dma, dma,
+            vmem((INNER, MID, 128), BF16), vmem((INNER, MID, 128), BF16), dma, dma,
+            vmem((INNER, 1, 384), F32), vmem((INNER, 1, 384), F32), vmem((RG, 1, 128), F32), dma((2,)), dma((2,)),
             vmem((32, 128), BF16), vmem((GG, 32, 128), BF16), dma, dma,
             vmem((16, 128), BF16), vmem((RG, 16, 128), BF16), dma, dma,
-            vmem((RG, 32, 128), BF16), dma, dma,
+            vmem((RG, 16, 128), BF16), dma, dma,
             pltpu.SemaphoreType.REGULAR((2,)),
             vmem((PAIRS, ROWS, 128), F32), vmem((ROWS, 128), F32), vmem((PAIRS, MID, 128), F32),
             vmem((256, 128), F32), vmem((256, 128), F32),
@@ -445,7 +468,7 @@
     return pl.pallas_call(
         merge,
         out_shape=pltpu.HBM((ROWS, 1024), BF16),
-        in_specs=[pl.BlockSpec(memory_space=pltpu.VMEM)] * 3,
+        in_specs=[pl.BlockSpec(memory_space=pltpu.VMEM)] * 4,
         out_specs=pl.BlockSpec(memory_space=pltpu.HBM),
         scratch_shapes=[
             vmem((FAR, 16, 1024), BF16), dma((2 * FAR,)),

time: 21.6 us -> 21 us (0.972)
  Pallas kernels: 21.5 us -> 20.9 us
    pallas_call x1, Pallas kernels: 20.5 us -> 19.9 us  [on_device(): pl.pallas_call(kernel, out_shape=[vmem((ROWS, 1024), BF16), vmem((2, 16,...]
where the time goes in v5:
time: 21 us; the launch traced here: 20.9 us
  Pallas kernels  20.9 us (100%)
    pallas_call x1, Pallas kernels, on_device(): pl.pallas_call(kernel, out_shape=[vmem((ROWS, 1024), BF16), vmem((2, 16,...  19.9 us
    pallas_call x1, Pallas kernels, on_device(): pl.pallas_call(merge, out_shape=pltpu.HBM((ROWS, 1024), BF16), in_specs=[...  0.99 us

profile of v5, /device:TPU:1, one launch (start us, length us, event | category | flops | bytes accessed | tf_op | source)
XLA Modules:
  0.0 20.9 jit_solution(10935657102694537345)
XLA Ops:
  0.0 19.9 %shard_map.37 = (bf16[512,1024]{1,0:T(8,128)(2,1)S(1)}, f32[2,16,128]{2,1,0:T(8,128)S(1)}, bf16[16,16,128]{2,1,0:T(8,128)(2,1)S(1)}, f32[16,1,128]{2,1,0:T(1,128)S(1)}) custom-call(bf16[512,1024]{1,0:T(8,128)(2,1)} %q_hbm.1, bf16[512,1024]{1,0:T(8,128)(2,1)} %k_hbm.1, bf16[512,1024]{1,0:T(8,128)(2,1)} %v_hbm.1), custom_call_target="tpu_custom_call" | custom-call | tf_op jit(solution)/shard_map/pallas_call | solution.py:443
  19.9 1.0 %shard_map.38 = bf16[512,1024]{1,0:T(8,128)(2,1)} custom-call(bf16[512,1024]{1,0:T(8,128)(2,1)S(1)} %get-tuple-element.9.merged_ref, f32[2,16,128]{2,1,0:T(8,128)S(1)} %get-tuple-element.10.two_ref, bf16[16,16,128]{2,1,0:T(8,128)(2,1)S(1)} %get-tuple-element.11.far_recv, f32[16,1,128]{2,1,0:T(1,128)S(1)} %get-tuple-element.12.far_lse_recv), custom_call_target="tpu_custom_call" | custom-call | tf_op jit(solution)/shard_map/pallas_call | solution.py:468

commit v6 on v5

--- a/solution.py
+++ b/solution.py
@@ -128,12 +128,22 @@
     at_along_late = jnp.where(z < 4, at_mid - wave + wave // 3, -1)
 
     barrier = pltpu.get_barrier_semaphore()
+    def speak_along(peers):
+        for who, later, _ in peers:
+            @pl.when(jnp.logical_and(later >= 0, later < 9))
+            def _(who=who):
+                pl.semaphore_signal(barrier, 1, device_id=who, device_id_type=MESH)
+
+    @pl.when(z >= 4)
+    def _():
+        speak_along(along[8:])
+
     for who in near:
         pl.semaphore_signal(barrier, 1, device_id=who, device_id_type=MESH)
-    for who, later, _ in along:
-        @pl.when(jnp.logical_and(later >= 0, later < 9))
-        def _(who=who):
-            pl.semaphore_signal(barrier, 1, device_id=who, device_id_type=MESH)
+
+    @pl.when(z < 4)
+    def _():
+        speak_along(along)
 
     edges = []
     for a, src in ((1, k_hbm), (2, v_hbm), (0, q_hbm)):
@@ -193,7 +203,7 @@
             wide = ref[:, columns].astype(F32)
             if a == 0:
                 wide = wide * 0.125
-            stage[a] = wide
+            stage[a, 0:ROWS, :] = wide
         for a in range(3):
             one = stage[a, pl.ds(first_row, MID, stride=8), :]
             two = stage[a, pl.ds(first_row + 1, MID, stride=8), :]
@@ -228,17 +238,21 @@
                 kv_copy(who).start()
 
     def send_mid():
-        @pl.when(opens > 0)
-        def _():
-            for who in near[:7]:
-                mid_copy(who).start()
-
         for copy in edges[4:]:
             copy.wait()
         pick_edge(0)
         fq_send[...] = (far_stage[0] * 0.125).astype(BF16)
         fq_recv[my_near] = fq_send[...]
-        for who in near:
+        distant = near[:3] + near[7:9]
+        for who in distant:
+            fq_copy(who).start()
+
+        @pl.when(opens > 0)
+        def _():
+            for who in near[:7]:
+                mid_copy(who).start()
+
+        for who in near[3:7] + near[9:]:
             fq_copy(who).start()
 
     def send_along(half):
@@ -285,7 +299,7 @@
         stage[1, 0:256, :] = fq_recv[...].reshape(256, 128).astype(F32)
         got = kv_recv.at[pl.ds(0, GG - 1)]
         pltpu.make_async_copy(got, got, kv_rsem).wait()
-        stage[0] = kv_recv[...].reshape(ROWS, 128).astype(F32)
+        stage[0, 0:ROWS, :] = kv_recv[...].reshape(ROWS, 128).astype(F32)
         scores, blocks = [], []
         for p in range(PAIRS):
             q = jnp.concatenate([stage[1, pl.ds(2 * p + t, RG, stride=16), :] for t in range(FAR)], axis=0)
@@ -377,7 +391,7 @@
             two_ref[1, 2 * p + t : 2 * p + t + 1, :] = lse[row : row + 1]
         att_ref[p, pl.ds(first_row, MID, stride=8), :] = jnp.where(second, one, merged)
         att_ref[p, pl.ds(first_row + 1, MID, stride=8), :] = jnp.where(second, merged, two)
-        merged_ref[:, 128 * p : 128 * p + 128] = att_ref[p].astype(BF16)
+        merged_ref[:, 128 * p : 128 * p + 128] = att_ref[p, 0:ROWS, :].astype(BF16)
 
     sent = mid_send.at[pl.ds(0, INNER - 1)]
     pltpu.make_async_copy(sent, sent, mid_ssem).wait()
@@ -450,7 +464,7 @@
         scratch_shapes=[
             vmem((ROWS, 1024), BF16), vmem((ROWS, 1024), BF16), vmem((ROWS, 1024), BF16),
             vmem((3, FAR, 16, 1024), BF16), dma((3,)), dma((3, FAR)),
-            vmem((3, ROWS, 128), F32), vmem((3, 16, 128), F32),
+            vmem((3, ROWS + 32, 128), F32), vmem((3, 16, 128), F32),
             vmem((INNER, 3 * MID, 128), BF16), vmem((INNER, 3 * MID, 128), BF16), dma, dma,
             vmem((INNER, MID, 128), BF16), vmem((INNER, MID, 128), BF16), dma, dma,
             vmem((INNER, 1, 384), F32), vmem((INNER, 1, 384), F32), vmem((RG, 1, 128), F32), dma((2,)), dma((2,)),
@@ -458,8 +472,8 @@
             vmem((16, 128), BF16), vmem((RG, 16, 128), BF16), dma, dma,
             vmem((RG, 16, 128), BF16), dma, dma,
             pltpu.SemaphoreType.REGULAR((2,)),
-            vmem((PAIRS, ROWS, 128), F32), vmem((ROWS, 128), F32), vmem((PAIRS, MID, 128), F32),
-            vmem((256, 128), F32), vmem((256, 128), F32),
+            vmem((PAIRS, ROWS + 8, 128), F32), vmem((ROWS + 8, 128), F32), vmem((PAIRS, MID, 128), F32),
+            vmem((256 + 16, 128), F32), vmem((256 + 16, 128), F32),
         ],
         compiler_params=pltpu.CompilerParams(
             collective_id=0, has_side_effects=True, vmem_limit_bytes=40 * 1024 * 1024

time: 21 us -> 20.8 us (level)
  Pallas kernels: 20.9 us -> 20.5 us
    pallas_call x1, Pallas kernels: 19.9 us -> 19.5 us  [on_device(): pl.pallas_call(kernel, out_shape=[vmem((ROWS, 1024), BF16), vmem((2, 16,...]
where the time goes in v6:
time: 20.8 us; the launch traced here: 20.5 us
  Pallas kernels  20.5 us (99%)
    pallas_call x1, Pallas kernels, on_device(): pl.pallas_call(kernel, out_shape=[vmem((ROWS, 1024), BF16), vmem((2, 16,...  19.5 us
    pallas_call x1, Pallas kernels, on_device(): pl.pallas_call(merge, out_shape=pltpu.HBM((ROWS, 1024), BF16), in_specs=[...  0.99 us

profile of v6, /device:TPU:1, one launch (start us, length us, event | category | flops | bytes accessed | tf_op | source)
XLA Modules:
  0.0 20.5 jit_solution(12437301229218606518)
XLA Ops:
  0.0 19.5 %shard_map.37 = (bf16[512,1024]{1,0:T(8,128)(2,1)S(1)}, f32[2,16,128]{2,1,0:T(8,128)S(1)}, bf16[16,16,128]{2,1,0:T(8,128)(2,1)S(1)}, f32[16,1,128]{2,1,0:T(1,128)S(1)}) custom-call(bf16[512,1024]{1,0:T(8,128)(2,1)} %q_hbm.1, bf16[512,1024]{1,0:T(8,128)(2,1)} %k_hbm.1, bf16[512,1024]{1,0:T(8,128)(2,1)} %v_hbm.1), custom_call_target="tpu_custom_call" | custom-call | tf_op jit(solution)/shard_map/pallas_call | solution.py:457
  19.6 1.0 %shard_map.38 = bf16[512,1024]{1,0:T(8,128)(2,1)} custom-call(bf16[512,1024]{1,0:T(8,128)(2,1)S(1)} %get-tuple-element.9.merged_ref, f32[2,16,128]{2,1,0:T(8,128)S(1)} %get-tuple-element.10.two_ref, bf16[16,16,128]{2,1,0:T(8,128)(2,1)S(1)} %get-tuple-element.11.far_recv, f32[16,1,128]{2,1,0:T(1,128)S(1)} %get-tuple-element.12.far_lse_recv), custom_call_target="tpu_custom_call" | custom-call | tf_op jit(solution)/shard_map/pallas_call | solution.py:482

commit v7 on v5

--- a/solution.py
+++ b/solution.py
@@ -193,7 +193,7 @@
             wide = ref[:, columns].astype(F32)
             if a == 0:
                 wide = wide * 0.125
-            stage[a] = wide
+            stage[a, 0:ROWS, :] = wide
         for a in range(3):
             one = stage[a, pl.ds(first_row, MID, stride=8), :]
             two = stage[a, pl.ds(first_row + 1, MID, stride=8), :]
@@ -285,7 +285,7 @@
         stage[1, 0:256, :] = fq_recv[...].reshape(256, 128).astype(F32)
         got = kv_recv.at[pl.ds(0, GG - 1)]
         pltpu.make_async_copy(got, got, kv_rsem).wait()
-        stage[0] = kv_recv[...].reshape(ROWS, 128).astype(F32)
+        stage[0, 0:ROWS, :] = kv_recv[...].reshape(ROWS, 128).astype(F32)
         scores, blocks = [], []
         for p in range(PAIRS):
             q = jnp.concatenate([stage[1, pl.ds(2 * p + t, RG, stride=16), :] for t in range(FAR)], axis=0)
@@ -377,7 +377,7 @@
             two_ref[1, 2 * p + t : 2 * p + t + 1, :] = lse[row : row + 1]
         att_ref[p, pl.ds(first_row, MID, stride=8), :] = jnp.where(second, one, merged)
         att_ref[p, pl.ds(first_row + 1, MID, stride=8), :] = jnp.where(second, merged, two)
-        merged_ref[:, 128 * p : 128 * p + 128] = att_ref[p].astype(BF16)
+        merged_ref[:, 128 * p : 128 * p + 128] = att_ref[p, 0:ROWS, :].astype(BF16)
 
     sent = mid_send.at[pl.ds(0, INNER - 1)]
     pltpu.make_async_copy(sent, sent, mid_ssem).wait()
@@ -450,7 +450,7 @@
         scratch_shapes=[
             vmem((ROWS, 1024), BF16), vmem((ROWS, 1024), BF16), vmem((ROWS, 1024), BF16),
             vmem((3, FAR, 16, 1024), BF16), dma((3,)), dma((3, FAR)),
-            vmem((3, ROWS, 128), F32), vmem((3, 16, 128), F32),
+            vmem((3, ROWS + 32, 128), F32), vmem((3, 16, 128), F32),
             vmem((INNER, 3 * MID, 128), BF16), vmem((INNER, 3 * MID, 128), BF16), dma, dma,
             vmem((INNER, MID, 128), BF16), vmem((INNER, MID, 128), BF16), dma, dma,
             vmem((INNER, 1, 384), F32), vmem((INNER, 1, 384), F32), vmem((RG, 1, 128), F32), dma((2,)), dma((2,)),
@@ -458,8 +458,8 @@
             vmem((16, 128), BF16), vmem((RG, 16, 128), BF16), dma, dma,
             vmem((RG, 16, 128), BF16), dma, dma,
             pltpu.SemaphoreType.REGULAR((2,)),
-            vmem((PAIRS, ROWS, 128), F32), vmem((ROWS, 128), F32), vmem((PAIRS, MID, 128), F32),
-            vmem((256, 128), F32), vmem((256, 128), F32),
+            vmem((PAIRS, ROWS + 8, 128), F32), vmem((ROWS + 8, 128), F32), vmem((PAIRS, MID, 128), F32),
+            vmem((256 + 16, 128), F32), vmem((256 + 16, 128), F32),
         ],
         compiler_params=pltpu.CompilerParams(
             collective_id=0, has_side_effects=True, vmem_limit_bytes=40 * 1024 * 1024

time: 21 us -> 21 us (level)
  no operation moved by 1% of the time
where the time goes in v7:
time: 21 us; the launch traced here: 20.9 us
  Pallas kernels  20.9 us (100%)
    pallas_call x1, Pallas kernels, on_device(): pl.pallas_call(kernel, out_shape=[vmem((ROWS, 1024), BF16), vmem((2, 16,...  19.9 us
    pallas_call x1, Pallas kernels, on_device(): pl.pallas_call(merge, out_shape=pltpu.HBM((ROWS, 1024), BF16), in_specs=[...  0.99 us

profile of v7, /device:TPU:1, one launch (start us, length us, event | category | flops | bytes accessed | tf_op | source)
XLA Modules:
  0.0 20.9 jit_solution(13426328684862098022)
XLA Ops:
  0.0 19.9 %shard_map.37 = (bf16[512,1024]{1,0:T(8,128)(2,1)S(1)}, f32[2,16,128]{2,1,0:T(8,128)S(1)}, bf16[16,16,128]{2,1,0:T(8,128)(2,1)S(1)}, f32[16,1,128]{2,1,0:T(1,128)S(1)}) custom-call(bf16[512,1024]{1,0:T(8,128)(2,1)} %q_hbm.1, bf16[512,1024]{1,0:T(8,128)(2,1)} %k_hbm.1, bf16[512,1024]{1,0:T(8,128)(2,1)} %v_hbm.1), custom_call_target="tpu_custom_call" | custom-call | tf_op jit(solution)/shard_map/pallas_call | solution.py:443
  19.9 1.0 %shard_map.38 = bf16[512,1024]{1,0:T(8,128)(2,1)} custom-call(bf16[512,1024]{1,0:T(8,128)(2,1)S(1)} %get-tuple-element.9.merged_ref, f32[2,16,128]{2,1,0:T(8,128)S(1)} %get-tuple-element.10.two_ref, bf16[16,16,128]{2,1,0:T(8,128)(2,1)S(1)} %get-tuple-element.11.far_recv, f32[16,1,128]{2,1,0:T(1,128)S(1)} %get-tuple-element.12.far_lse_recv), custom_call_target="tpu_custom_call" | custom-call | tf_op jit(solution)/shard_map/pallas_call | solution.py:468

commit v8 on v6

--- a/solution.py
+++ b/solution.py
@@ -238,21 +238,17 @@
                 kv_copy(who).start()
 
     def send_mid():
+        @pl.when(opens > 0)
+        def _():
+            for who in near[:7]:
+                mid_copy(who).start()
+
         for copy in edges[4:]:
             copy.wait()
         pick_edge(0)
         fq_send[...] = (far_stage[0] * 0.125).astype(BF16)
         fq_recv[my_near] = fq_send[...]
-        distant = near[:3] + near[7:9]
-        for who in distant:
-            fq_copy(who).start()
-
-        @pl.when(opens > 0)
-        def _():
-            for who in near[:7]:
-                mid_copy(who).start()
-
-        for who in near[3:7] + near[9:]:
+        for who in near:
             fq_copy(who).start()
 
     def send_along(half):

time: 20.8 us -> 21 us (level)
  Pallas kernels: 20.5 us -> 20.9 us
    pallas_call x1, Pallas kernels: 19.5 us -> 19.9 us  [on_device(): pl.pallas_call(kernel, out_shape=[vmem((ROWS, 1024), BF16), vmem((2, 16,...]
where the time goes in v8:
time: 21 us; the launch traced here: 20.9 us
  Pallas kernels  20.9 us (100%)
    pallas_call x1, Pallas kernels, on_device(): pl.pallas_call(kernel, out_shape=[vmem((ROWS, 1024), BF16), vmem((2, 16,...  19.9 us
    pallas_call x1, Pallas kernels, on_device(): pl.pallas_call(merge, out_shape=pltpu.HBM((ROWS, 1024), BF16), in_specs=[...  0.99 us

profile of v8, /device:TPU:1, one launch (start us, length us, event | category | flops | bytes accessed | tf_op | source)
XLA Modules:
  0.0 20.9 jit_solution(6747900405696736200)
XLA Ops:
  0.0 19.9 %shard_map.37 = (bf16[512,1024]{1,0:T(8,128)(2,1)S(1)}, f32[2,16,128]{2,1,0:T(8,128)S(1)}, bf16[16,16,128]{2,1,0:T(8,128)(2,1)S(1)}, f32[16,1,128]{2,1,0:T(1,128)S(1)}) custom-call(bf16[512,1024]{1,0:T(8,128)(2,1)} %q_hbm.1, bf16[512,1024]{1,0:T(8,128)(2,1)} %k_hbm.1, bf16[512,1024]{1,0:T(8,128)(2,1)} %v_hbm.1), custom_call_target="tpu_custom_call" | custom-call | tf_op jit(solution)/shard_map/pallas_call | solution.py:453
  19.9 1.0 %shard_map.38 = bf16[512,1024]{1,0:T(8,128)(2,1)} custom-call(bf16[512,1024]{1,0:T(8,128)(2,1)S(1)} %get-tuple-element.9.merged_ref, f32[2,16,128]{2,1,0:T(8,128)S(1)} %get-tuple-element.10.two_ref, bf16[16,16,128]{2,1,0:T(8,128)(2,1)S(1)} %get-tuple-element.11.far_recv, f32[16,1,128]{2,1,0:T(1,128)S(1)} %get-tuple-element.12.far_lse_recv), custom_call_target="tpu_custom_call" | custom-call | tf_op jit(solution)/shard_map/pallas_call | solution.py:478
